TPU v7x, 32 devices: a whole 2x2x4 slice. The times are simulated.
32 devices in a mesh: sub: 16 (over z, y, x), rhs: 2 (over core).
Axes of the slice: x: 2, y: 2, z: 4, core: 2. Of those that a mesh axis runs over, the one named last changes fastest.
Arguments:
- schur_block: bfloat16 [32, 1024, 1024], P('sub', 'rhs'), may hold values from -1 to 4, as said below
- scaling: float32 [32, 1024], P('sub'), may hold values from 0.25 to 1.75
- gravity_load: float32 [32, 1024, 256], P('sub', None, 'rhs'), may hold values from -100 to 100
- pressure: bfloat16 [1024, 4, 256], P('sub', None, 'rhs'), may hold values from -6 to 6
- block_target: int32 [1024, 1], P('sub'), may hold values from 0 to 31; in each aligned block of 64 rows (0 to 63, 64 to 127, ...) at most 4 rows name the same one
- aero_interp: float32 [4, 1024], replicated, may hold values from -0.5 to 0.5
- partner_slot: int32 [4, 32], P(None, 'sub'), may hold values from 0 to 1, as said below
- corner_row: int32 [32, 8], P('sub'), may hold values from 0 to 1023
- corner_coarse: int32 [32, 8], P('sub'), may hold values from 0 to 127
- coarse_inverse: float32 [128, 128], P('sub'), may hold values from -1 to 6, as said below
Outputs:
- solution: float32 [32, 1024, 256], P('sub', None, 'rhs')
Inputs may be any that keep to these rules, and one draw needn't show every extreme that they name: `block_target`: at most 4 of the blocks of one device name the same subdomain; in some device's blocks one subdomain is named exactly 4 times; every subdomain is named by some block. In round k, subdomain s on device d = s // 2 is paired with subdomain (d xor 2^k) * 2 + partner_slot[k, s]; the pairing is mutual. `schur_block`: each matrix is symmetric. `coarse_inverse`: symmetric.
All inputs are finite; a program needn't handle non-finite values.
Results may differ from a plain program's by a relative error of at most 0.0027.
Values may be sent and summed in bfloat16 or wider, within the bound.
A program may use at most 64 MiB of HBM per device.

v0:
```python
import jax
import jax.numpy as jnp
from jax import lax
from jax.sharding import PartitionSpec as P

SUB_DEV = 2
FACES = 4
MOST = 4
ITERS = 2
FW = 256


coupling = 2.0


def swapped(shard, axis, distance):
    return lax.ppermute(shard, axis, [(i, i ^ 1 << distance) for i in range(lax.axis_size(axis))])


def schur_apply(schur_block, rounded):
    half_rows = jnp.einsum(
        "snm,smc->snc",
        schur_block,
        lax.all_gather(rounded, "rhs", axis=2, tiled=True),
        preferred_element_type=jnp.float32,
    )
    return lax.all_to_all(half_rows, "rhs", split_axis=2, concat_axis=1, tiled=True)


def jump_terms(rounded, partner_slot):
    face_terms = []
    for face_index in range(FACES):
        own_face = rounded[:, face_index * FW : (face_index + 1) * FW, :]
        partner_face = swapped(own_face, "sub", face_index)
        select = (
            partner_slot[face_index][:, None] == jnp.arange(SUB_DEV, dtype=jnp.int32)[None, :]
        ).astype(jnp.bfloat16)
        picked = jnp.einsum("sj,jfc->sfc", select, partner_face, preferred_element_type=jnp.float32)
        face_terms.append(coupling * (own_face.astype(jnp.float32) - picked))
    return jnp.concatenate(face_terms, axis=1)


def operator(direction, schur_block, partner_slot):
    rounded = direction.astype(jnp.bfloat16)
    return schur_apply(schur_block, rounded) + jump_terms(rounded, partner_slot)


def coarse_solve(coarse, coarse_inverse):
    own_rows = jnp.dot(coarse_inverse, coarse, precision=lax.Precision.HIGHEST)
    return lax.all_gather(own_rows, "sub", axis=0, tiled=True)


def add_corners(solved, corner_row, corner_coarse, residual):
    sub_rows = jnp.arange(SUB_DEV, dtype=jnp.int32)[:, None]
    return jnp.zeros_like(residual).at[sub_rows, corner_row].add(solved[corner_coarse])


def precondition(residual, schur_block, scaling, corner_row, corner_coarse, coarse_inverse):
    columns = residual.shape[2]
    weight_col = scaling[:, :, None]
    dirichlet = weight_col * schur_apply(schur_block, (weight_col * residual).astype(jnp.bfloat16))
    sub_rows = jnp.arange(SUB_DEV, dtype=jnp.int32)[:, None]
    picked = residual[sub_rows, corner_row]
    partial_sum = (
        jnp.zeros((coarse_inverse.shape[1], columns), jnp.float32)
        .at[corner_coarse.reshape(-1)]
        .add(picked.reshape(-1, columns))
    )
    coarse = lax.psum(partial_sum, "sub")
    solved = coarse_solve(coarse, coarse_inverse)
    precond = dirichlet + add_corners(solved, corner_row, corner_coarse, residual)
    product_value = lax.psum(jnp.sum(residual * precond, axis=(0, 1)), "sub")
    return (precond, product_value)


def on_device(
    schur_block,
    scaling,
    gravity_load,
    pressure,
    block_target,
    aero_interp,
    partner_slot,
    corner_row,
    corner_coarse,
    coarse_inverse,
):
    sub_count = lax.axis_size("sub")
    all_subdomains = SUB_DEV * sub_count
    columns = gravity_load.shape[2]
    points = pressure.shape[1]
    target = block_target[:, 0]
    matches = target[:, None] == target[None, :]
    before = jnp.tril(matches, -1)
    rank_in = jnp.sum(before, axis=1, dtype=jnp.int32)
    slot_index = target * MOST + rank_in
    buffer = (
        jnp.zeros((all_subdomains * MOST, points, columns), jnp.bfloat16)
        .at[slot_index]
        .set(pressure)
    )
    arrived = lax.all_to_all(buffer, "sub", split_axis=0, concat_axis=0, tiled=True)
    load_sum = jnp.sum(
        arrived.reshape(sub_count, SUB_DEV, MOST, points, columns), axis=(0, 2), dtype=jnp.float32
    )
    force_total = gravity_load + jnp.einsum(
        "pm,spc->smc", aero_interp, load_sum, precision=lax.Precision.HIGHEST
    )
    solution = jnp.zeros_like(force_total)
    residual = force_total
    precond, precond_dot = precondition(
        residual, schur_block, scaling, corner_row, corner_coarse, coarse_inverse
    )
    direction = precond
    for step_index in range(ITERS):
        applied = operator(direction, schur_block, partner_slot)
        curvature = lax.psum(jnp.sum(direction * applied, axis=(0, 1)), "sub")
        step_size = precond_dot / curvature
        solution = solution + step_size * direction
        residual = residual - step_size * applied
        if step_index + 1 < ITERS:
            precond, next_product = precondition(
                residual, schur_block, scaling, corner_row, corner_coarse, coarse_inverse
            )
            direction = precond + next_product / precond_dot * direction
            precond_dot = next_product
    return solution


def solution(mesh):
    return jax.shard_map(
        on_device,
        mesh=mesh,
        in_specs=(
            P("sub", "rhs", None),
            P("sub", None),
            P("sub", None, "rhs"),
            P("sub", None, "rhs"),
            P("sub", None),
            P(),
            P(None, "sub"),
            P("sub", None),
            P("sub", None),
            P("sub", None),
        ),
        out_specs=P("sub", None, "rhs"),
        check_vma=False,
    )
```

profile of v0, /device:TPU:0, one launch (start us, length us, event | category | flops | bytes accessed | tf_op | source)
XLA Modules:
  0.0 575.1 jit_solution(14376807275874382460)
XLA Ops:
  9.7 7.6 %scatter_fusion = bf16[128,4,128]{2,1,0:T(4,128)(2,1)} fusion(bf16[128,4,128]{2,1,0:T(4,128)(2,1)} %broadcast_in_dim.12, s32[64]{0:T(128)S(1)} %fusion.22, bf16[64,4,128]{2,1,0:T(4,128)(2,1)} %param.13), kind=kCustom, calls=%fused_computation.4 | custom fusion | bytes 196864 | tf_op jit(solution)/shard_map/scatter | solution.py:100
  17.3 8.3 %all-to-all-start = ((bf16[128,4,128]{2,1,0:T(4,128)(2,1)}), bf16[128,4,128]{2,1,0:T(4,128)(2,1)S(1)}, u32[]{:S(2)}, u32[]{:S(2)}) async-start(bf16[128,4,128]{2,1,0:T(4,128)(2,1)} %scatter_fusion), calls=%async_computation | async-start | bytes 262144 | tf_op jit(solution)/shard_map/all_to_all | solution.py:102
  27.2 2.5 copy.107
  29.7 3.7 all-to-all-done
  33.5 3.1 multiply_convert_fusion.1
  40.8 98.9 %all-reduce.4.cloned.1.call-done = f32[128,128]{1,0:T(8,128)} async-done(((f32[128,128]{1,0:T(8,128)}), f32[128,128]{1,0:T(8,128)}) %all-reduce.4.cloned.1.call-update) | async-done | bytes 65552 | tf_op jit(solution)/shard_map/psum | solution.py:69
  140.7 39.1 %all_gather.19 = f32[128,128]{1,0:T(8,128)S(1)} all-gather(f32[8,128]{1,0:T(8,128)S(1)} %convolution_bitcast_fusion.6), channel_id=1, replica_groups=mesh['sub'=16,'rhs'=2] {'sub'}, dimensions={0}, use_global_device_ids=true | all-gather | bytes 69632 | tf_op jit(solution)/shard_map/all_gather | solution.py:50
  183.3 4.6 all_to_all.77
  192.9 2.6 copy.111
  195.5 2.2 scatter_fusion.1
  204.5 3.0 collective-permute-done
  220.8 2.3 subtract_multiply_fusion.7
  226.0 4.6 all_to_all.78
  232.3 3.2 all_to_all.63
  237.6 39.5 %all-reduce = (f32[128]{0:T(128)S(1)}, f32[128]{0:T(128)S(1)}) all-reduce(f32[128]{0:T(128)S(1)} %get-tuple-element.6, f32[128]{0:T(128)S(1)} %get-tuple-element.5), channel_id=1, replica_groups=mesh['sub'=16,'rhs'=2] {'sub'}, use_global_device_ids=true, to_apply=%region_7.8 | all-reduce | flops 256 | bytes 2048 | tf_op jit(solution)/shard_map/psum | solution.py:72
  277.1 3.3 multiply_convert_fusion
  280.3 2.5 copy.128
  285.7 97.4 %all-reduce.6.cloned.1.call-done = f32[128,128]{1,0:T(8,128)} async-done(((f32[128,128]{1,0:T(8,128)}), f32[128,128]{1,0:T(8,128)}) %all-reduce.6.cloned.1.call-update) | async-done | bytes 65552 | tf_op jit(solution)/shard_map/psum | solution.py:69
  384.0 39.1 %all_gather.22 = f32[128,128]{1,0:T(8,128)S(1)} all-gather(f32[8,128]{1,0:T(8,128)S(1)} %convolution_bitcast_fusion.5), channel_id=1, replica_groups=mesh['sub'=16,'rhs'=2] {'sub'}, dimensions={0}, use_global_device_ids=true | all-gather | bytes 69632 | tf_op jit(solution)/shard_map/all_gather | solution.py:50
  426.6 4.6 all_to_all.79
  433.0 3.1 all_to_all.67
  436.1 2.4 broadcast_multiply_fusion
  438.5 2.6 copy.129
  443.3 2.5 copy.130
  447.5 36.9 %psum.46 = f32[128]{0:T(128)S(1)} all-reduce(f32[128]{0:T(128)S(1)} %multiply_reduce_fusion), channel_id=1, replica_groups=mesh['sub'=16,'rhs'=2] {'sub'}, use_global_device_ids=true, to_apply=%region_14.15 | all-reduce | flops 128 | bytes 1024 | tf_op jit(solution)/shard_map/psum | solution.py:72
  484.4 2.2 fusion.32
  507.3 2.3 subtract_multiply_fusion.3
  512.4 4.6 all_to_all.80
  518.8 3.2 all_to_all.71
  524.0 38.5 %psum.47 = f32[128]{0:T(128)S(1)} all-reduce(f32[128]{0:T(128)S(1)} %fusion.2), channel_id=1, replica_groups=mesh['sub'=16,'rhs'=2] {'sub'}, use_global_device_ids=true, to_apply=%region_16.17 | all-reduce | flops 128 | bytes 1024 | tf_op jit(solution)/shard_map/psum | solution.py:117
  562.5 2.5 multiply_add_fusion
  565.0 2.5 copy.143
  (135 shorter events, 84.6 us)
Async XLA Ops:
  7.4 173.1 %copy-start = (bf16[2,512,1024]{2,1,0:T(8,128)(2,1)S(1)}, bf16[2,512,1024]{2,1,0:T(8,128)(2,1)}, u32[]{:S(2)}) copy-start(bf16[2,512,1024]{2,1,0:T(8,128)(2,1)} %param.10) | copy-start | bytes 6291460
  7.4 26.1 %copy-start.2 = (f32[2,1024]{1,0:T(2,128)S(1)}, f32[2,1024]{1,0:T(2,128)}, u32[]{:S(2)}) copy-start(f32[2,1024]{1,0:T(2,128)} %param.11) | copy-start | bytes 24580
  7.4 26.1 %copy-start.5 = (f32[4,1024]{1,0:T(4,128)S(1)}, f32[4,1024]{1,0:T(4,128)}, u32[]{:S(2)}) copy-start(f32[4,1024]{1,0:T(4,128)} %param.15) | copy-start | bytes 49156
  17.3 16.1 %all-to-all-start = ((bf16[128,4,128]{2,1,0:T(4,128)(2,1)}), bf16[128,4,128]{2,1,0:T(4,128)(2,1)S(1)}, u32[]{:S(2)}, u32[]{:S(2)}) async-start(bf16[128,4,128]{2,1,0:T(4,128)(2,1)} %scatter_fusion), calls=%async_computation | async-start | bytes 262144 | tf_op jit(solution)/shard_map/all_to_all | solution.py:102
  25.6 114.1 %all-reduce.4.cloned.1.call-start = ((), (), s32[]{:S(2)}) async-start(), calls=%async_computation.6 | async-start | bytes 131072 | tf_op jit(solution)/shard_map/psum | solution.py:69
  27.2 10.7 %copy-start.13 = (s32[16]{0:T(128)}, s32[16]{0:T(128)S(1)}, u32[]{:S(2)}) copy-start(s32[16]{0:T(128)S(1)} %reshape.57) | copy-start | bytes 196
  29.7 8.2 %copy-start.14 = (s32[16]{0:T(128)}, s32[16]{0:T(128)S(1)}, u32[]{:S(2)}) copy-start(s32[16]{0:T(128)S(1)} %fusion.23) | copy-start | bytes 196
  33.5 7.1 %copy-start.9 = (s32[2,8]{1,0:T(2,128)S(1)}, s32[2,8]{1,0:T(2,128)}, u32[]{:S(2)}) copy-start(s32[2,8]{1,0:T(2,128)} %param.18) | copy-start | bytes 196
  33.5 106.2 %copy-start.3 = (f32[8,128]{1,0:T(8,128)S(1)}, f32[8,128]{1,0:T(8,128)}, u32[]{:S(2)}) copy-start(f32[8,128]{1,0:T(8,128)} %param.19) | copy-start | bytes 12292
  36.6 145.8 %copy-start.1 = (f32[2,1024,128]{1,2,0:T(8,128)}, f32[2,1024,128]{1,2,0:T(8,128)S(1)}, u32[]{:S(2)}) copy-start(f32[2,1024,128]{1,2,0:T(8,128)S(1)} %get-tuple-element.34) | copy-start | bytes 3145732
  40.0 140.4 %all-gather.5.cloned.1.call-start = ((), (), s32[]{:S(2)}) async-start(), calls=%async_computation.5 | async-start | bytes 1572864 | tf_op jit(solution)/shard_map/all_gather | solution.py:24
  40.6 182.6 %all-gather.7.cloned.1.call-start = ((), (), s32[]{:S(2)}) async-start(), calls=%async_computation.7 | async-start | bytes 1572864 | tf_op jit(solution)/shard_map/all_gather | solution.py:24
  40.8 141.6 %copy-start.6 = (s32[1024]{0:T(1024)}, s32[1024]{0:T(1024)S(1)}, u32[]{:S(2)}) copy-start(s32[1024]{0:T(1024)S(1)} %pad_clamp_fusion) | copy-start | bytes 12292
  197.6 4.3 copy-start.4
  201.9 5.5 collective-permute-start
  202.8 180.3 %all-reduce.6.cloned.1.call-start = ((), (), s32[]{:S(2)}) async-start(), calls=%async_computation.9 | async-start | bytes 131072 | tf_op jit(solution)/shard_map/psum | solution.py:69
  203.0 7.3 %collective-permute-start.3 = (bf16[2,256,128]{1,2,0:T(8,128)(2,1)}, bf16[2,256,128]{1,2,0:T(8,128)(2,1)}, u32[]{:S(2)}, u32[]{:S(2)}) collective-permute-start(bf16[2,256,128]{1,2,0:T(8,128)(2,1)} %get-tuple-element.28), channel_id=1, source_target_pairs={{0,16},{2,18},{4,20},{6,22},{8,24},{10,26},{12,28},{14,30},{16,0},... | collective-permute-start | bytes 393224 | tf_op jit(solution)/shard_map/ppermute | solution.py:17
  203.1 11.1 %collective-permute-start.2 = (bf16[2,256,128]{1,2,0:T(8,128)(2,1)}, bf16[2,256,128]{1,2,0:T(8,128)(2,1)}, u32[]{:S(2)}, u32[]{:S(2)}) collective-permute-start(bf16[2,256,128]{1,2,0:T(8,128)(2,1)} %get-tuple-element.29), channel_id=1, source_target_pairs={{0,8},{2,10},{4,12},{6,14},{8,0},{10,2},{12,4},{14,6},{16,24},{18,... | collective-permute-start | bytes 393224 | tf_op jit(solution)/shard_map/ppermute | solution.py:17
  203.2 14.8 %collective-permute-start.1 = (bf16[2,256,128]{1,2,0:T(8,128)(2,1)}, bf16[2,256,128]{1,2,0:T(8,128)(2,1)S(1)}, u32[]{:S(2)}, u32[]{:S(2)}) collective-permute-start(bf16[2,256,128]{1,2,0:T(8,128)(2,1)} %get-tuple-element.30), channel_id=1, source_target_pairs={{0,4},{2,6},{4,0},{6,2},{8,12},{10,14},{12,8},{14,10},{16,20},{18,... | collective-permute-start | bytes 393224 | tf_op jit(solution)/shard_map/ppermute | solution.py:17
  277.1 3.3 copy-start.7
  285.0 138.8 %all-gather.9.cloned.1.call-start = ((), (), s32[]{:S(2)}) async-start(), calls=%async_computation.8 | async-start | bytes 1572864 | tf_op jit(solution)/shard_map/all_gather | solution.py:24
  285.6 224.0 %all-gather.11.cloned.1.call-start = ((), (), s32[]{:S(2)}) async-start(), calls=%async_computation.10 | async-start | bytes 1572864 | tf_op jit(solution)/shard_map/all_gather | solution.py:24
  484.4 4.0 copy-start.15
  486.6 11.9 %copy-start.12 = (s32[2]{0:T(128)S(1)}, s32[2]{0:T(128)}, u32[]{:S(2)}) copy-start(s32[2]{0:T(128)} %get-tuple-element.9) | copy-start | bytes 28
  486.6 15.7 %copy-start.11 = (s32[2]{0:T(128)S(1)}, s32[2]{0:T(128)}, u32[]{:S(2)}) copy-start(s32[2]{0:T(128)} %get-tuple-element.10) | copy-start | bytes 28
  488.5 5.0 collective-permute-start.4
  490.5 6.4 %collective-permute-start.7 = (bf16[2,256,128]{1,2,0:T(8,128)(2,1)}, bf16[2,256,128]{1,2,0:T(8,128)(2,1)}, u32[]{:S(2)}, u32[]{:S(2)}) collective-permute-start(bf16[2,256,128]{1,2,0:T(8,128)(2,1)} %get-tuple-element.20), channel_id=1, source_target_pairs={{0,16},{2,18},{4,20},{6,22},{8,24},{10,26},{12,28},{14,30},{16,0},... | collective-permute-start | bytes 393224 | tf_op jit(solution)/shard_map/ppermute | solution.py:17
  490.6 10.1 %collective-permute-start.6 = (bf16[2,256,128]{1,2,0:T(8,128)(2,1)}, bf16[2,256,128]{1,2,0:T(8,128)(2,1)}, u32[]{:S(2)}, u32[]{:S(2)}) collective-permute-start(bf16[2,256,128]{1,2,0:T(8,128)(2,1)} %get-tuple-element.21), channel_id=1, source_target_pairs={{0,8},{2,10},{4,12},{6,14},{8,0},{10,2},{12,4},{14,6},{16,24},{18,... | collective-permute-start | bytes 393224 | tf_op jit(solution)/shard_map/ppermute | solution.py:17
  490.7 14.5 %copy-start.10 = (s32[2]{0:T(128)S(1)}, s32[2]{0:T(128)}, u32[]{:S(2)}) copy-start(s32[2]{0:T(128)} %get-tuple-element.8) | copy-start | bytes 28
  490.7 13.7 %collective-permute-start.5 = (bf16[2,256,128]{1,2,0:T(8,128)(2,1)}, bf16[2,256,128]{1,2,0:T(8,128)(2,1)S(1)}, u32[]{:S(2)}, u32[]{:S(2)}) collective-permute-start(bf16[2,256,128]{1,2,0:T(8,128)(2,1)} %get-tuple-element.22), channel_id=1, source_target_pairs={{0,4},{2,6},{4,0},{6,2},{8,12},{10,14},{12,8},{14,10},{16,20},{18,... | collective-permute-start | bytes 393224 | tf_op jit(solution)/shard_map/ppermute | solution.py:17
  521.9 40.6 %copy-start.16 = (f32[128]{0:T(128)S(1)}, f32[128]{0:T(128)}, u32[]{:S(2)}) copy-start(f32[128]{0:T(128)} %copy-done.15) | copy-start | bytes 1540
  521.9 40.6 %copy-start.8 = (f32[128]{0:T(128)S(1)}, f32[128]{0:T(128)}, u32[]{:S(2)}) copy-start(f32[128]{0:T(128)} %copy-done.7) | copy-start | bytes 1540
Sparse Core Ops, SparseCore 0:
  40.1 99.5 all-reduce.3
  285.1 97.8 all-reduce.5
Sparse Core Ops, SparseCore 1:
  42.0 6.5 all-gather.4
  202.9 6.7 all-gather.6
  287.1 4.7 all-gather.8
  490.6 5.2 all-gather.10
where the time goes:
time: 577 us; the launch traced here: 575 us
  blocking collectives  211 us (37%)
  waiting for transfers between devices  206 us (36%)
  local copies, waits for them, and re-layouts  71.8 us (12%)
  other arithmetic  33.9 us (6%)
  matrix products  23 us (4%)
  between operations  15.4 us (3%)
  starting transfers between devices  13.9 us (2%)
    psum x2, waiting for transfers between devices, precondition(): coarse = lax.psum(partial_sum, 'sub')  196 us
    all_gather x2, blocking collectives, coarse_solve(): return lax.all_gather(own_rows, 'sub', axis=0, tiled=True)  78.2 us
    psum x2, blocking collectives, precondition(): product_value = lax.psum(jnp.sum(residual * precond, axis=(0, 1)), 'sub')  76.4 us
    psum x1, blocking collectives, on_device(): curvature = lax.psum(jnp.sum(direction * applied, axis=(0, 1)), 'sub')  38.5 us
    all_to_all x8, local copies, waits for them, and re-layouts, schur_apply(): lax.all_to_all(half_rows, 'rhs', split_axis=2, concat_axis=1, tiled=True)  18.7 us
    all_to_all x4, blocking collectives, schur_apply(): lax.all_to_all(half_rows, 'rhs', split_axis=2, concat_axis=1, tiled=True)  18.3 us
  transfers between devices with their start and end apart: 15, of which 6 were waited for; matrix products, arithmetic and copies ran while one was open for 7% of the time, Pallas kernels for 0%

commit v1 on v0

--- a/solution.py
+++ b/solution.py
@@ -15,6 +15,14 @@
 
 def swapped(shard, axis, distance):
     return lax.ppermute(shard, axis, [(i, i ^ 1 << distance) for i in range(lax.axis_size(axis))])
+
+
+def all_sum(value):
+    distance = 0
+    while 1 << distance < lax.axis_size("sub"):
+        value = value + swapped(value, "sub", distance)
+        distance += 1
+    return value
 
 
 def schur_apply(schur_block, rounded):
@@ -47,7 +55,9 @@
 
 def coarse_solve(coarse, coarse_inverse):
     own_rows = jnp.dot(coarse_inverse, coarse, precision=lax.Precision.HIGHEST)
-    return lax.all_gather(own_rows, "sub", axis=0, tiled=True)
+    start = lax.axis_index("sub") * own_rows.shape[0]
+    whole = jnp.zeros_like(coarse)
+    return all_sum(lax.dynamic_update_slice(whole, own_rows, (start, 0)))
 
 
 def add_corners(solved, corner_row, corner_coarse, residual):
@@ -66,10 +76,10 @@
         .at[corner_coarse.reshape(-1)]
         .add(picked.reshape(-1, columns))
     )
-    coarse = lax.psum(partial_sum, "sub")
+    coarse = all_sum(partial_sum)
     solved = coarse_solve(coarse, coarse_inverse)
     precond = dirichlet + add_corners(solved, corner_row, corner_coarse, residual)
-    product_value = lax.psum(jnp.sum(residual * precond, axis=(0, 1)), "sub")
+    product_value = all_sum(jnp.sum(residual * precond, axis=(0, 1)))
     return (precond, product_value)
 
 
@@ -114,7 +124,7 @@
     direction = precond
     for step_index in range(ITERS):
         applied = operator(direction, schur_block, partner_slot)
-        curvature = lax.psum(jnp.sum(direction * applied, axis=(0, 1)), "sub")
+        curvature = all_sum(jnp.sum(direction * applied, axis=(0, 1)))
         step_size = precond_dot / curvature
         solution = solution + step_size * direction
         residual = residual - step_size * applied

time: 577 us -> 295 us (0.51)
  blocking collectives: 211 us -> 18.3 us
  waiting for transfers between devices: 206 us -> 87.4 us
  starting transfers between devices: 13.9 us -> 55.2 us
    psum x2 -> x0, waiting for transfers between devices: 196 us -> none  [precondition(): coarse = lax.psum(partial_sum, 'sub')]
    psum x3 -> x0, blocking collectives: 115 us -> none  [the longest x2 76.4 us: precondition(): product_value = lax.psum(jnp.sum(residual * precond, axis=(0, 1)), 'sub')]
    ppermute x8 -> x40, waiting for transfers between devices: 4.7 us -> 82.9 us  [swapped(): lax.ppermute(shard, axis, [(i, i ^ 1 << distance) for i in range(lax.axis...]
    all_gather x2 -> x0, blocking collectives: 78.2 us -> none  [coarse_solve(): return lax.all_gather(own_rows, 'sub', axis=0, tiled=True)]
    ppermute x8 -> x40, starting transfers between devices: 5.18 us -> 46.5 us  [swapped(): lax.ppermute(shard, axis, [(i, i ^ 1 << distance) for i in range(lax.axis...]
  transfers between devices with their start and end apart: 15 -> 45, of which waited for: 6 -> 34; matrix products, arithmetic and copies ran while one was open for 7% -> 14% of each run, Pallas kernels for 0% -> 0%
where the time goes in v1:
time: 295 us; the launch traced here: 293 us
  waiting for transfers between devices  87.4 us (30%)
  local copies, waits for them, and re-layouts  67.7 us (23%)
  starting transfers between devices  55.2 us (19%)
  other arithmetic  29.9 us (10%)
  matrix products  21.3 us (7%)
  blocking collectives  18.3 us (6%)
  between operations  13.5 us (5%)
    ppermute x40, waiting for transfers between devices, swapped(): lax.ppermute(shard, axis, [(i, i ^ 1 << distance) for i in range(lax.axis...  82.9 us
    ppermute x40, starting transfers between devices, swapped(): lax.ppermute(shard, axis, [(i, i ^ 1 << distance) for i in range(lax.axis...  46.5 us
    all_to_all x4, blocking collectives, schur_apply(): lax.all_to_all(half_rows, 'rhs', split_axis=2, concat_axis=1, tiled=True)  18.3 us
    all_to_all x8, local copies, waits for them, and re-layouts, schur_apply(): lax.all_to_all(half_rows, 'rhs', split_axis=2, concat_axis=1, tiled=True)  17.4 us
    dot_general x8, matrix products, jump_terms(): jnp.einsum('sj,jfc->sfc', select, partner_face, preferred_element_type=jn...  10.1 us
    ppermute x8, local copies, waits for them, and re-layouts, swapped(): lax.ppermute(shard, axis, [(i, i ^ 1 << distance) for i in range(lax.axis...  9.77 us
    all_to_all x1, starting transfers between devices, on_device(): lax.all_to_all(buffer, 'sub', split_axis=0, concat_axis=0, tiled=True)  8.36 us
    dot_general x4, matrix products, schur_apply(): jnp.einsum('snm,smc->snc', schur_block, lax.all_gather(rounded, 'rhs', ax...  7.88 us
  transfers between devices with their start and end apart: 45, of which 34 were waited for; matrix products, arithmetic and copies ran while one was open for 14% of the time, Pallas kernels for 0%

profile of v1, /device:TPU:0, one launch (start us, length us, event | category | flops | bytes accessed | tf_op | source)
XLA Modules:
  0.0 293.4 jit_solution(6070715701411228412)
XLA Ops:
  8.9 6.8 %scatter_fusion = bf16[128,4,128]{2,1,0:T(4,128)(2,1)} fusion(bf16[128,4,128]{2,1,0:T(4,128)(2,1)} %broadcast_in_dim.12, s32[64]{0:T(128)S(1)} %fusion.24, bf16[64,4,128]{2,1,0:T(4,128)(2,1)} %param.13), kind=kCustom, calls=%fused_computation.4 | custom fusion | bytes 196864 | tf_op jit(solution)/shard_map/scatter | solution.py:110
  15.7 8.4 %all-to-all-start = ((bf16[128,4,128]{2,1,0:T(4,128)(2,1)}), bf16[128,4,128]{2,1,0:T(4,128)(2,1)S(1)}, u32[]{:S(2)}, u32[]{:S(2)}) async-start(bf16[128,4,128]{2,1,0:T(4,128)(2,1)} %scatter_fusion), calls=%async_computation | async-start | bytes 262144 | tf_op jit(solution)/shard_map/all_to_all | solution.py:112
  24.8 2.5 copy.107
  27.5 4.4 %all-to-all-done = bf16[128,4,128]{2,1,0:T(4,128)(2,1)S(1)} async-done(((bf16[128,4,128]{2,1,0:T(4,128)(2,1)}), bf16[128,4,128]{2,1,0:T(4,128)(2,1)S(1)}, u32[]{:S(2)}, u32[]{:S(2)}) %all-to-all-start) | async-done | bytes 131104 | tf_op jit(solution)/shard_map/all_to_all | solution.py:112
  32.0 3.1 %multiply_convert_fusion.1 = (bf16[2,1024,128]{1,2,0:T(8,128)(2,1)}, f32[2,1024,128]{1,2,0:T(8,128)S(1)}) fusion(f32[2,1024]{1,0:T(2,128)S(1)} %copy-done.9, f32[2,1024,128]{1,2,0:T(8,128)} %copy.107, f32[2,4,128]{2,1,0:T(4,128)S(1)} %convert_reduce_fusion, f32[4,1024]{1,0:T(4,128)S(1)} %copy-done.12), kind=kOutput, calls=%fused_computation.32 | convolution fusion | flops 13369344 | bytes 2650112 | tf_op jit(solution)/shard_map/pm,spc->smc/dot_general | solution.py:116
  39.0 3.2 %collective-permute-done = f32[128,128]{1,0:T(8,128)S(1)} collective-permute-done((f32[128,128]{1,0:T(8,128)S(1)}, f32[128,128]{1,0:T(8,128)S(1)}, u32[]{:S(2)}, u32[]{:S(2)}) %collective-permute-start) | collective-permute-done | bytes 65568 | tf_op jit(solution)/shard_map/ppermute | solution.py:17
  43.0 3.5 %collective-permute-done.1 = f32[128,128]{1,0:T(8,128)S(1)} collective-permute-done((f32[128,128]{1,0:T(8,128)S(1)}, f32[128,128]{1,0:T(8,128)S(1)}, u32[]{:S(2)}, u32[]{:S(2)}) %collective-permute-start.1) | collective-permute-done | bytes 65568 | tf_op jit(solution)/shard_map/ppermute | solution.py:17
  47.4 3.8 %collective-permute-done.2 = f32[128,128]{1,0:T(8,128)S(1)} collective-permute-done((f32[128,128]{1,0:T(8,128)S(1)}, f32[128,128]{1,0:T(8,128)S(1)}, u32[]{:S(2)}, u32[]{:S(2)}) %collective-permute-start.2) | collective-permute-done | bytes 65568 | tf_op jit(solution)/shard_map/ppermute | solution.py:17
  52.0 5.0 %collective-permute-done.3 = f32[128,128]{1,0:T(8,128)S(1)} collective-permute-done((f32[128,128]{1,0:T(8,128)S(1)}, f32[128,128]{1,0:T(8,128)S(1)}, u32[]{:S(2)}, u32[]{:S(2)}) %collective-permute-start.3) | collective-permute-done | bytes 65568 | tf_op jit(solution)/shard_map/ppermute | solution.py:17
  58.0 3.4 %collective-permute-done.4 = f32[128,128]{1,0:T(8,128)S(1)} collective-permute-done((f32[128,128]{1,0:T(8,128)S(1)}, f32[128,128]{1,0:T(8,128)S(1)}, u32[]{:S(2)}, u32[]{:S(2)}) %collective-permute-start.4) | collective-permute-done | bytes 65568 | tf_op jit(solution)/shard_map/ppermute | solution.py:17
  62.2 3.5 %collective-permute-done.5 = f32[128,128]{1,0:T(8,128)S(1)} collective-permute-done((f32[128,128]{1,0:T(8,128)S(1)}, f32[128,128]{1,0:T(8,128)S(1)}, u32[]{:S(2)}, u32[]{:S(2)}) %collective-permute-start.5) | collective-permute-done | bytes 65568 | tf_op jit(solution)/shard_map/ppermute | solution.py:17
  66.0 4.1 %collective-permute-done.6 = f32[128,128]{1,0:T(8,128)S(1)} collective-permute-done((f32[128,128]{1,0:T(8,128)S(1)}, f32[128,128]{1,0:T(8,128)S(1)}, u32[]{:S(2)}, u32[]{:S(2)}) %collective-permute-start.6) | collective-permute-done | bytes 65568 | tf_op jit(solution)/shard_map/ppermute | solution.py:17
  70.4 5.1 %collective-permute-done.7 = f32[128,128]{1,0:T(8,128)S(1)} collective-permute-done((f32[128,128]{1,0:T(8,128)S(1)}, f32[128,128]{1,0:T(8,128)S(1)}, u32[]{:S(2)}, u32[]{:S(2)}) %collective-permute-start.7) | collective-permute-done | bytes 65568 | tf_op jit(solution)/shard_map/ppermute | solution.py:17
  78.9 4.6 %all_to_all.77 = f32[2,512,256]{1,0,2:T(2,128)S(1)} all-to-all(f32[2,512,256]{1,0,2:T(2,128)S(1)} %copy.108), channel_id=1, replica_groups=mesh['sub'=16,'rhs'=2] {'rhs'}, dimensions={2} | all-to-all | bytes 2097152 | tf_op jit(solution)/shard_map/all_to_all | solution.py:35
  119.4 4.6 %all_to_all.78 = f32[2,512,256]{1,0,2:T(2,128)S(1)} all-to-all(f32[2,512,256]{1,0,2:T(2,128)S(1)} %copy.114), channel_id=1, replica_groups=mesh['sub'=16,'rhs'=2] {'rhs'}, dimensions={2} | all-to-all | bytes 2097152 | tf_op jit(solution)/shard_map/all_to_all | solution.py:35
  125.8 3.1 %all_to_all.63 = f32[2,1024,128]{1,2,0:T(8,128)} reshape(f32[2,2,512,128]{2,1,3,0:T(2,128)} %bitcast.106) | data formatting | bytes 2097152 | tf_op jit(solution)/shard_map/all_to_all | solution.py:35
  149.3 2.5 copy.128
  154.6 3.1 %collective-permute-done.20 = f32[128,128]{1,0:T(8,128)S(1)} collective-permute-done((f32[128,128]{1,0:T(8,128)S(1)}, f32[128,128]{1,0:T(8,128)S(1)}, u32[]{:S(2)}, u32[]{:S(2)}) %collective-permute-start.20) | collective-permute-done | bytes 65568 | tf_op jit(solution)/shard_map/ppermute | solution.py:17
  159.0 3.1 %collective-permute-done.21 = f32[128,128]{1,0:T(8,128)S(1)} collective-permute-done((f32[128,128]{1,0:T(8,128)S(1)}, f32[128,128]{1,0:T(8,128)S(1)}, u32[]{:S(2)}, u32[]{:S(2)}) %collective-permute-start.21) | collective-permute-done | bytes 65568 | tf_op jit(solution)/shard_map/ppermute | solution.py:17
  163.5 2.9 collective-permute-done.22
  168.6 3.1 %collective-permute-done.23 = f32[128,128]{1,0:T(8,128)S(1)} collective-permute-done((f32[128,128]{1,0:T(8,128)S(1)}, f32[128,128]{1,0:T(8,128)S(1)}, u32[]{:S(2)}, u32[]{:S(2)}) %collective-permute-start.23) | collective-permute-done | bytes 65568 | tf_op jit(solution)/shard_map/ppermute | solution.py:17
  173.0 3.1 %collective-permute-done.24 = f32[128,128]{1,0:T(8,128)S(1)} collective-permute-done((f32[128,128]{1,0:T(8,128)S(1)}, f32[128,128]{1,0:T(8,128)S(1)}, u32[]{:S(2)}, u32[]{:S(2)}) %collective-permute-start.24) | collective-permute-done | bytes 65568 | tf_op jit(solution)/shard_map/ppermute | solution.py:17
  177.3 3.1 %collective-permute-done.25 = f32[128,128]{1,0:T(8,128)S(1)} collective-permute-done((f32[128,128]{1,0:T(8,128)S(1)}, f32[128,128]{1,0:T(8,128)S(1)}, u32[]{:S(2)}, u32[]{:S(2)}) %collective-permute-start.25) | collective-permute-done | bytes 65568 | tf_op jit(solution)/shard_map/ppermute | solution.py:17
  181.9 2.9 collective-permute-done.26
  186.9 3.1 %collective-permute-done.27 = f32[128,128]{1,0:T(8,128)S(1)} collective-permute-done((f32[128,128]{1,0:T(8,128)S(1)}, f32[128,128]{1,0:T(8,128)S(1)}, u32[]{:S(2)}, u32[]{:S(2)}) %collective-permute-start.27) | collective-permute-done | bytes 65568 | tf_op jit(solution)/shard_map/ppermute | solution.py:17
  193.5 4.6 %all_to_all.79 = f32[2,512,256]{1,0,2:T(2,128)S(1)} all-to-all(f32[2,512,256]{1,0,2:T(2,128)S(1)} %copy.126), channel_id=1, replica_groups=mesh['sub'=16,'rhs'=2] {'rhs'}, dimensions={2} | all-to-all | bytes 2097152 | tf_op jit(solution)/shard_map/all_to_all | solution.py:35
  199.9 3.1 %all_to_all.67 = f32[2,1024,128]{1,2,0:T(8,128)} reshape(f32[2,2,512,128]{2,1,3,0:T(2,128)} %bitcast.108) | data formatting | bytes 2097152 | tf_op jit(solution)/shard_map/all_to_all | solution.py:35
  205.3 2.5 copy.129
  210.1 2.6 copy.130
  256.2 4.6 %all_to_all.80 = f32[2,512,256]{1,0,2:T(2,128)S(1)} all-to-all(f32[2,512,256]{1,0,2:T(2,128)S(1)} %copy.133), channel_id=1, replica_groups=mesh['sub'=16,'rhs'=2] {'rhs'}, dimensions={2} | all-to-all | bytes 2097152 | tf_op jit(solution)/shard_map/all_to_all | solution.py:35
  262.6 3.1 %all_to_all.71 = f32[2,1024,128]{1,2,0:T(8,128)} reshape(f32[2,2,512,128]{2,1,3,0:T(2,128)} %bitcast.110) | data formatting | bytes 2097152 | tf_op jit(solution)/shard_map/all_to_all | solution.py:35
  280.2 2.7 collective-permute-done.39
  (226 shorter events, 160.8 us)
Async XLA Ops:
  15.7 16.2 %all-to-all-start = ((bf16[128,4,128]{2,1,0:T(4,128)(2,1)}), bf16[128,4,128]{2,1,0:T(4,128)(2,1)S(1)}, u32[]{:S(2)}, u32[]{:S(2)}) async-start(bf16[128,4,128]{2,1,0:T(4,128)(2,1)} %scatter_fusion), calls=%async_computation | async-start | bytes 262144 | tf_op jit(solution)/shard_map/all_to_all | solution.py:112
  24.1 52.0 %all-gather.5.cloned.1.call-start = ((), (), s32[]{:S(2)}) async-start(), calls=%async_computation.5 | async-start | bytes 1572864 | tf_op jit(solution)/shard_map/all_gather | solution.py:32
  37.9 4.3 %collective-permute-start = (f32[128,128]{1,0:T(8,128)S(1)}, f32[128,128]{1,0:T(8,128)S(1)}, u32[]{:S(2)}, u32[]{:S(2)}) collective-permute-start(f32[128,128]{1,0:T(8,128)S(1)} %scatter_custom_fusion.1), channel_id=1, source_target_pairs={{0,2},{2,0},{4,6},{6,4},{8,10},{10,8},{12,14},{14,12},{16,18},{18,... | collective-permute-start | bytes 196616 | tf_op jit(solution)/shard_map/ppermute | solution.py:17
  42.2 4.3 %collective-permute-start.1 = (f32[128,128]{1,0:T(8,128)S(1)}, f32[128,128]{1,0:T(8,128)S(1)}, u32[]{:S(2)}, u32[]{:S(2)}) collective-permute-start(f32[128,128]{1,0:T(8,128)S(1)} %add.182), channel_id=1, source_target_pairs={{0,4},{2,6},{4,0},{6,2},{8,12},{10,14},{12,8},{14,10},{16,20},{18,... | collective-permute-start | bytes 196616 | tf_op jit(solution)/shard_map/ppermute | solution.py:17
  46.6 4.7 %collective-permute-start.2 = (f32[128,128]{1,0:T(8,128)S(1)}, f32[128,128]{1,0:T(8,128)S(1)}, u32[]{:S(2)}, u32[]{:S(2)}) collective-permute-start(f32[128,128]{1,0:T(8,128)S(1)} %add.183), channel_id=1, source_target_pairs={{0,8},{2,10},{4,12},{6,14},{8,0},{10,2},{12,4},{14,6},{16,24},{18,... | collective-permute-start | bytes 196616 | tf_op jit(solution)/shard_map/ppermute | solution.py:17
  47.4 69.3 %all-gather.7.cloned.1.call-start = ((), (), s32[]{:S(2)}) async-start(), calls=%async_computation.6 | async-start | bytes 1572864 | tf_op jit(solution)/shard_map/all_gather | solution.py:32
  51.3 5.8 %collective-permute-start.3 = (f32[128,128]{1,0:T(8,128)S(1)}, f32[128,128]{1,0:T(8,128)S(1)}, u32[]{:S(2)}, u32[]{:S(2)}) collective-permute-start(f32[128,128]{1,0:T(8,128)S(1)} %add.184), channel_id=1, source_target_pairs={{0,16},{2,18},{4,20},{6,22},{8,24},{10,26},{12,28},{14,30},{16,0},... | collective-permute-start | bytes 196616 | tf_op jit(solution)/shard_map/ppermute | solution.py:17
  57.2 4.3 %collective-permute-start.4 = (f32[128,128]{1,0:T(8,128)S(1)}, f32[128,128]{1,0:T(8,128)S(1)}, u32[]{:S(2)}, u32[]{:S(2)}) collective-permute-start(f32[128,128]{1,0:T(8,128)S(1)} %get-tuple-element.37), channel_id=1, source_target_pairs={{0,2},{2,0},{4,6},{6,4},{8,10},{10,8},{12,14},{14,12},{16,18},{18,... | collective-permute-start | bytes 196616 | tf_op jit(solution)/shard_map/ppermute | solution.py:17
  65.8 4.3 %collective-permute-start.6 = (f32[128,128]{1,0:T(8,128)S(1)}, f32[128,128]{1,0:T(8,128)S(1)}, u32[]{:S(2)}, u32[]{:S(2)}) collective-permute-start(f32[128,128]{1,0:T(8,128)S(1)} %add.188), channel_id=1, source_target_pairs={{0,8},{2,10},{4,12},{6,14},{8,0},{10,2},{12,4},{14,6},{16,24},{18,... | collective-permute-start | bytes 196616 | tf_op jit(solution)/shard_map/ppermute | solution.py:17
  70.1 5.4 %collective-permute-start.7 = (f32[128,128]{1,0:T(8,128)S(1)}, f32[128,128]{1,0:T(8,128)S(1)}, u32[]{:S(2)}, u32[]{:S(2)}) collective-permute-start(f32[128,128]{1,0:T(8,128)S(1)} %add.189), channel_id=1, source_target_pairs={{0,16},{2,18},{4,20},{6,22},{8,24},{10,26},{12,28},{14,30},{16,0},... | collective-permute-start | bytes 196616 | tf_op jit(solution)/shard_map/ppermute | solution.py:17
  95.4 5.5 %collective-permute-start.12 = (bf16[2,256,128]{1,2,0:T(8,128)(2,1)S(1)}, bf16[2,256,128]{1,2,0:T(8,128)(2,1)S(1)}, u32[]{:S(2)}, u32[]{:S(2)}) collective-permute-start(bf16[2,256,128]{1,2,0:T(8,128)(2,1)S(1)} %get-tuple-element.29), channel_id=1, source_target_pairs={{0,2},{2,0},{4,6},{6,4},{8,10},{10,8},{12,14},{14,12},{16,18},{18,... | collective-permute-start | bytes 393224 | tf_op jit(solution)/shard_map/ppermute | solution.py:17
  97.1 93.6 %all-gather.9.cloned.1.call-start = ((), (), s32[]{:S(2)}) async-start(), calls=%async_computation.7 | async-start | bytes 1572864 | tf_op jit(solution)/shard_map/all_gather | solution.py:32
  97.3 6.6 %collective-permute-start.13 = (bf16[2,256,128]{1,2,0:T(8,128)(2,1)}, bf16[2,256,128]{1,2,0:T(8,128)(2,1)}, u32[]{:S(2)}, u32[]{:S(2)}) collective-permute-start(bf16[2,256,128]{1,2,0:T(8,128)(2,1)} %get-tuple-element.32), channel_id=1, source_target_pairs={{0,4},{2,6},{4,0},{6,2},{8,12},{10,14},{12,8},{14,10},{16,20},{18,... | collective-permute-start | bytes 393224 | tf_op jit(solution)/shard_map/ppermute | solution.py:17
  97.8 9.8 %collective-permute-start.14 = (bf16[2,256,128]{1,2,0:T(8,128)(2,1)}, bf16[2,256,128]{1,2,0:T(8,128)(2,1)}, u32[]{:S(2)}, u32[]{:S(2)}) collective-permute-start(bf16[2,256,128]{1,2,0:T(8,128)(2,1)} %get-tuple-element.31), channel_id=1, source_target_pairs={{0,8},{2,10},{4,12},{6,14},{8,0},{10,2},{12,4},{14,6},{16,24},{18,... | collective-permute-start | bytes 393224 | tf_op jit(solution)/shard_map/ppermute | solution.py:17
  97.8 13.6 %collective-permute-start.15 = (bf16[2,256,128]{1,2,0:T(8,128)(2,1)}, bf16[2,256,128]{1,2,0:T(8,128)(2,1)S(1)}, u32[]{:S(2)}, u32[]{:S(2)}) collective-permute-start(bf16[2,256,128]{1,2,0:T(8,128)(2,1)} %get-tuple-element.30), channel_id=1, source_target_pairs={{0,16},{2,18},{4,20},{6,22},{8,24},{10,26},{12,28},{14,30},{16,0},... | collective-permute-start | bytes 393224 | tf_op jit(solution)/shard_map/ppermute | solution.py:17
  141.8 4.4 %collective-permute-start.19 = (f32[128]{0:T(128)S(1)}, f32[128]{0:T(128)S(1)}, u32[]{:S(2)}, u32[]{:S(2)}) collective-permute-start(f32[128]{0:T(128)S(1)} %add.199), channel_id=1, source_target_pairs={{0,16},{2,18},{4,20},{6,22},{8,24},{10,26},{12,28},{14,30},{16,0},... | collective-permute-start | bytes 1544 | tf_op jit(solution)/shard_map/ppermute | solution.py:17
  142.7 4.4 %collective-permute-start.11 = (f32[128]{0:T(128)S(1)}, f32[128]{0:T(128)S(1)}, u32[]{:S(2)}, u32[]{:S(2)}) collective-permute-start(f32[128]{0:T(128)S(1)} %add.194), channel_id=1, source_target_pairs={{0,16},{2,18},{4,20},{6,22},{8,24},{10,26},{12,28},{14,30},{16,0},... | collective-permute-start | bytes 1544 | tf_op jit(solution)/shard_map/ppermute | solution.py:17
  149.2 104.2 %all-gather.11.cloned.1.call-start = ((), (), s32[]{:S(2)}) async-start(), calls=%async_computation.8 | async-start | bytes 1572864 | tf_op jit(solution)/shard_map/all_gather | solution.py:32
  153.4 4.3 %collective-permute-start.20 = (f32[128,128]{1,0:T(8,128)S(1)}, f32[128,128]{1,0:T(8,128)S(1)}, u32[]{:S(2)}, u32[]{:S(2)}) collective-permute-start(f32[128,128]{1,0:T(8,128)S(1)} %scatter_custom_fusion.3), channel_id=1, source_target_pairs={{0,2},{2,0},{4,6},{6,4},{8,10},{10,8},{12,14},{14,12},{16,18},{18,... | collective-permute-start | bytes 196616 | tf_op jit(solution)/shard_map/ppermute | solution.py:17
  157.7 4.3 %collective-permute-start.21 = (f32[128,128]{1,0:T(8,128)S(1)}, f32[128,128]{1,0:T(8,128)S(1)}, u32[]{:S(2)}, u32[]{:S(2)}) collective-permute-start(f32[128,128]{1,0:T(8,128)S(1)} %add.201), channel_id=1, source_target_pairs={{0,4},{2,6},{4,0},{6,2},{8,12},{10,14},{12,8},{14,10},{16,20},{18,... | collective-permute-start | bytes 196616 | tf_op jit(solution)/shard_map/ppermute | solution.py:17
  162.1 4.3 %collective-permute-start.22 = (f32[128,128]{1,0:T(8,128)S(1)}, f32[128,128]{1,0:T(8,128)S(1)}, u32[]{:S(2)}, u32[]{:S(2)}) collective-permute-start(f32[128,128]{1,0:T(8,128)S(1)} %add.202), channel_id=1, source_target_pairs={{0,8},{2,10},{4,12},{6,14},{8,0},{10,2},{12,4},{14,6},{16,24},{18,... | collective-permute-start | bytes 196616 | tf_op jit(solution)/shard_map/ppermute | solution.py:17
  166.4 5.2 %collective-permute-start.23 = (f32[128,128]{1,0:T(8,128)S(1)}, f32[128,128]{1,0:T(8,128)S(1)}, u32[]{:S(2)}, u32[]{:S(2)}) collective-permute-start(f32[128,128]{1,0:T(8,128)S(1)} %add.203), channel_id=1, source_target_pairs={{0,16},{2,18},{4,20},{6,22},{8,24},{10,26},{12,28},{14,30},{16,0},... | collective-permute-start | bytes 196616 | tf_op jit(solution)/shard_map/ppermute | solution.py:17
  171.8 4.3 %collective-permute-start.24 = (f32[128,128]{1,0:T(8,128)S(1)}, f32[128,128]{1,0:T(8,128)S(1)}, u32[]{:S(2)}, u32[]{:S(2)}) collective-permute-start(f32[128,128]{1,0:T(8,128)S(1)} %get-tuple-element.39), channel_id=1, source_target_pairs={{0,2},{2,0},{4,6},{6,4},{8,10},{10,8},{12,14},{14,12},{16,18},{18,... | collective-permute-start | bytes 196616 | tf_op jit(solution)/shard_map/ppermute | solution.py:17
  176.1 4.3 %collective-permute-start.25 = (f32[128,128]{1,0:T(8,128)S(1)}, f32[128,128]{1,0:T(8,128)S(1)}, u32[]{:S(2)}, u32[]{:S(2)}) collective-permute-start(f32[128,128]{1,0:T(8,128)S(1)} %add_dynamic-update-slice_fusion), channel_id=1, source_target_pairs={{0,4},{2,6},{4,0},{6,2},{8,12},{10,14},{12,8},{14,10},{16,20},{18,... | collective-permute-start | bytes 196616 | tf_op jit(solution)/shard_map/ppermute | solution.py:17
  180.4 4.3 %collective-permute-start.26 = (f32[128,128]{1,0:T(8,128)S(1)}, f32[128,128]{1,0:T(8,128)S(1)}, u32[]{:S(2)}, u32[]{:S(2)}) collective-permute-start(f32[128,128]{1,0:T(8,128)S(1)} %add.206), channel_id=1, source_target_pairs={{0,8},{2,10},{4,12},{6,14},{8,0},{10,2},{12,4},{14,6},{16,24},{18,... | collective-permute-start | bytes 196616 | tf_op jit(solution)/shard_map/ppermute | solution.py:17
  184.7 5.2 %collective-permute-start.27 = (f32[128,128]{1,0:T(8,128)S(1)}, f32[128,128]{1,0:T(8,128)S(1)}, u32[]{:S(2)}, u32[]{:S(2)}) collective-permute-start(f32[128,128]{1,0:T(8,128)S(1)} %add.207), channel_id=1, source_target_pairs={{0,16},{2,18},{4,20},{6,22},{8,24},{10,26},{12,28},{14,30},{16,0},... | collective-permute-start | bytes 196616 | tf_op jit(solution)/shard_map/ppermute | solution.py:17
  225.1 4.4 %collective-permute-start.31 = (f32[128]{0:T(128)S(1)}, f32[128]{0:T(128)S(1)}, u32[]{:S(2)}, u32[]{:S(2)}) collective-permute-start(f32[128]{0:T(128)S(1)} %add.211), channel_id=1, source_target_pairs={{0,16},{2,18},{4,20},{6,22},{8,24},{10,26},{12,28},{14,30},{16,0},... | collective-permute-start | bytes 1544 | tf_op jit(solution)/shard_map/ppermute | solution.py:17
  232.4 5.3 %collective-permute-start.32 = (bf16[2,256,128]{1,2,0:T(8,128)(2,1)S(1)}, bf16[2,256,128]{1,2,0:T(8,128)(2,1)S(1)}, u32[]{:S(2)}, u32[]{:S(2)}) collective-permute-start(bf16[2,256,128]{1,2,0:T(8,128)(2,1)S(1)} %get-tuple-element.21), channel_id=1, source_target_pairs={{0,2},{2,0},{4,6},{6,4},{8,10},{10,8},{12,14},{14,12},{16,18},{18,... | collective-permute-start | bytes 393224 | tf_op jit(solution)/shard_map/ppermute | solution.py:17
  233.6 7.0 %collective-permute-start.33 = (bf16[2,256,128]{1,2,0:T(8,128)(2,1)}, bf16[2,256,128]{1,2,0:T(8,128)(2,1)}, u32[]{:S(2)}, u32[]{:S(2)}) collective-permute-start(bf16[2,256,128]{1,2,0:T(8,128)(2,1)} %get-tuple-element.24), channel_id=1, source_target_pairs={{0,4},{2,6},{4,0},{6,2},{8,12},{10,14},{12,8},{14,10},{16,20},{18,... | collective-permute-start | bytes 393224 | tf_op jit(solution)/shard_map/ppermute | solution.py:17
  234.5 9.9 %collective-permute-start.34 = (bf16[2,256,128]{1,2,0:T(8,128)(2,1)}, bf16[2,256,128]{1,2,0:T(8,128)(2,1)}, u32[]{:S(2)}, u32[]{:S(2)}) collective-permute-start(bf16[2,256,128]{1,2,0:T(8,128)(2,1)} %get-tuple-element.23), channel_id=1, source_target_pairs={{0,8},{2,10},{4,12},{6,14},{8,0},{10,2},{12,4},{14,6},{16,24},{18,... | collective-permute-start | bytes 393224 | tf_op jit(solution)/shard_map/ppermute | solution.py:17
  236.3 11.9 %collective-permute-start.35 = (bf16[2,256,128]{1,2,0:T(8,128)(2,1)}, bf16[2,256,128]{1,2,0:T(8,128)(2,1)S(1)}, u32[]{:S(2)}, u32[]{:S(2)}) collective-permute-start(bf16[2,256,128]{1,2,0:T(8,128)(2,1)} %get-tuple-element.22), channel_id=1, source_target_pairs={{0,16},{2,18},{4,20},{6,22},{8,24},{10,26},{12,28},{14,30},{16,0},... | collective-permute-start | bytes 393224 | tf_op jit(solution)/shard_map/ppermute | solution.py:17
  278.5 4.4 %collective-permute-start.39 = (f32[128]{0:T(128)S(1)}, f32[128]{0:T(128)S(1)}, u32[]{:S(2)}, u32[]{:S(2)}) collective-permute-start(f32[128]{0:T(128)S(1)} %add.217), channel_id=1, source_target_pairs={{0,16},{2,18},{4,20},{6,22},{8,24},{10,26},{12,28},{14,30},{16,0},... | collective-permute-start | bytes 1544 | tf_op jit(solution)/shard_map/ppermute | solution.py:17
  (35 other events, 476.5 us)
Sparse Core Ops, SparseCore 0:
  47.5 6.6 all-gather.4
  97.2 7.4 all-gather.6
  149.4 7.6 all-gather.8
  233.8 8.9 all-gather.10

commit v2 on v0

v2 whole, which is shorter than its diff:
```python
import functools

import jax
import jax.numpy as jnp
from jax import lax
from jax.experimental import pallas as pl
from jax.experimental.pallas import tpu as pltpu
from jax.sharding import PartitionSpec as P

SUB_DEV = 2
FACES = 4
FW = 256
COUPLING = 2.0

MESH = pl.DeviceIdType.MESH
EXACT = lax.Precision.HIGHEST


def fold(value):
    return jnp.sum(value.reshape(-1, 8, value.shape[-1]), axis=0)


def kernel(
    n,
    chunks,
    schur,
    weight,
    gravity,
    loads,
    common,
    interp,
    spread,
    slots,
    corner_row,
    out,
    matrix,
    res,
    dirn,
    app,
    weighted,
    rounded,
    corner,
    mix,
    faces,
    picks_out,
    sums_out,
    dots_out,
    loads_in,
    common_in,
    picks_in,
    sums_in,
    dots_in,
    matrix_sem,
    face_send,
    face_recv,
    send_sem,
    recv_sem,
):
    me = lax.axis_index("sub")
    half = lax.axis_index("rhs")
    rows = schur.shape[1]
    corners = corner_row.shape[0] * corner_row.shape[1]
    per_sub = corner_row.shape[1]
    coarse_rows = common.shape[0] - corners
    blocks = gravity.shape[1] // FW
    half_blocks = rows // FW

    local = pltpu.make_async_copy(schur, matrix.at[half], matrix_sem.at[0])
    local.start()

    barrier = pltpu.get_barrier_semaphore()

    def greet(step, carry):
        pl.semaphore_signal(
            barrier, inc=1, device_id={"sub": lax.rem(me + step, n)}, device_id_type=MESH
        )
        return carry

    lax.fori_loop(1, n, greet, 0)
    pl.semaphore_signal(barrier, inc=1, device_id={"rhs": 1 - half}, device_id_type=MESH)
    pl.semaphore_wait(barrier, n)

    def send_all(which, source, target):
        def send(step, carry):
            peer = lax.rem(me + step, n)
            pltpu.make_async_remote_copy(
                src_ref=source(peer),
                dst_ref=target.at[me],
                send_sem=send_sem.at[which],
                recv_sem=recv_sem.at[which],
                device_id={"sub": peer},
                device_id_type=MESH,
            ).start()
            return carry

        lax.fori_loop(1, n, send, 0)
        target[me] = source(me)[...]

    def wait_all(sems, which, target):
        view = target.at[pl.ds(0, n - 1)]
        pltpu.make_async_copy(view, view, sems.at[which]).wait()

    send_all(0, lambda peer: loads.at[peer], loads_in)
    swap = pltpu.make_async_remote_copy(
        src_ref=schur,
        dst_ref=matrix.at[half],
        send_sem=matrix_sem.at[1],
        recv_sem=matrix_sem.at[2],
        device_id={"rhs": 1 - half},
        device_id_type=MESH,
    )
    send_all(1, lambda peer: common, common_in)
    swap.start()

    def tile(index):
        s, k = index // blocks, lax.rem(index, blocks)
        return s, k, pl.ds(pl.multiple_of(k * FW, FW), FW)

    def product(index, vector):
        s, k, _ = tile(index)
        part = pl.ds(pl.multiple_of(lax.rem(k, half_blocks) * FW, FW), FW)
        return jnp.dot(
            matrix[k // half_blocks, s, part, :], vector[s], preferred_element_type=jnp.float32
        )

    zero = jnp.zeros((8, out.shape[2]), jnp.float32)
    tiles = SUB_DEV * blocks

    def face_copy(turn, k):
        bit = 1 << k
        peer = me + bit - 2 * bit * lax.rem(me // bit, 2)
        return pltpu.make_async_remote_copy(
            src_ref=rounded.at[turn, :, pl.ds(k * FW, FW), :],
            dst_ref=faces.at[turn, k],
            send_sem=face_send.at[turn, k],
            recv_sem=face_recv.at[turn, k],
            device_id={"sub": peer},
            device_id_type=MESH,
        )

    def pick(source, target):
        for s in range(SUB_DEV):
            for i in range(per_sub):
                target[pl.ds(s * per_sub + i, 1), :] = source[s, pl.ds(corner_row[s, i], 1), :]

    def solve_corners(picked):
        solved = jnp.dot(mix[...], picked, precision=EXACT, preferred_element_type=jnp.float32)
        high = solved.astype(jnp.bfloat16).astype(jnp.float32)
        rest = solved - high
        middle = rest.astype(jnp.bfloat16).astype(jnp.float32)
        low = rest - middle
        for s in range(SUB_DEV):
            at = slice(s * per_sub, (s + 1) * per_sub)
            stack = [high[at], middle[at], low[at], jnp.zeros_like(low[at])]
            corner[s] = jnp.concatenate(stack, axis=0).astype(jnp.bfloat16)

    def corner_tile(s, at):
        return jnp.dot(spread[s, at, :], corner[s], preferred_element_type=jnp.float32)

    wait_all(recv_sem, 0, loads_in)
    load_sum = jnp.sum(loads_in[...], axis=0)

    def start_tile(index, carry):
        s, _, at = tile(index)
        force = gravity[s, at, :] + jnp.dot(
            interp[s, at, :], load_sum, precision=EXACT, preferred_element_type=jnp.float32
        )
        res[s, at, :] = force
        weighted[s, at, :] = (weight[s, at, :] * force).astype(jnp.bfloat16)
        return carry

    lax.fori_loop(0, tiles, start_tile, 0)
    pick(res, picks_out)
    send_all(2, lambda peer: picks_out, picks_in)

    wait_all(recv_sem, 1, common_in)
    lanes = common.shape[1]
    per_device = coarse_rows // chunks
    lane = lax.broadcasted_iota(jnp.int32, (1, lanes), 1).astype(jnp.float32)

    def one_hot(names, chunk):
        return jnp.where(names == lane + float(chunk * lanes), 1.0, 0.0).astype(jnp.float32)

    own = jnp.concatenate([one_hot(common[:corners], c) for c in range(chunks)], axis=1)
    names = common_in[:, :corners, :].reshape(n * corners, lanes)
    total = jnp.zeros((corners, n * corners), jnp.float32)
    for c in range(chunks):
        first = corners + c * per_device
        columns = common_in[:, first : first + per_device, :].reshape(n * per_device, lanes)
        left = jnp.dot(own, columns, precision=EXACT, preferred_element_type=jnp.float32)
        total += lax.dot_general(
            left,
            one_hot(names, c),
            (((1,), (1,)), ((), ())),
            precision=EXACT,
            preferred_element_type=jnp.float32,
        )
    mix[...] = total

    local.wait()
    swap.wait()

    def first_tile(index, carry):
        s, _, at = tile(index)
        dirn[s, at, :] = weight[s, at, :] * product(index, weighted)
        return carry

    lax.fori_loop(0, tiles, first_tile, 0)
    wait_all(recv_sem, 2, picks_in)
    picked = picks_in[...].reshape(n * corners, lanes)
    solve_corners(picked)

    acc = zero
    for k in reversed(range(FACES)):
        at = pl.ds(k * FW, FW)
        for s in range(SUB_DEV):
            value = dirn[s, at, :] + corner_tile(s, at)
            dirn[s, at, :] = value
            rounded[0, s, at, :] = value.astype(jnp.bfloat16)
            acc += fold(value * res[s, at, :])
        face_copy(0, k).start()
    own_dot = jnp.sum(acc, axis=0, keepdims=True)

    def apply(turn):
        def body(index, carry):
            s, _, at = tile(index)
            near = rounded[turn, s, at, :].astype(jnp.float32)
            app[s, at, :] = product(index, rounded.at[turn]) + COUPLING * near
            return carry

        lax.fori_loop(0, tiles, body, 0)
        acc = zero
        for k in range(FACES):
            face_copy(turn, k).wait_recv()
            at = pl.ds(k * FW, FW)
            for s in range(SUB_DEV):
                far = jnp.where(slots[k, s] == 0, faces[turn, k, 0], faces[turn, k, 1])
                far = far.astype(jnp.float32)
                value = app[s, at, :] - COUPLING * far
                if turn == 0:
                    app[s, at, :] = value
                acc += fold(value * dirn[s, at, :])
        return acc

    curvature = jnp.sum(apply(0), axis=0, keepdims=True)
    pick(app, sums_out)
    row = lax.broadcasted_iota(jnp.int32, (8, lanes), 0)
    sums_out[pl.ds(corners, 8), :] = jnp.where(
        row == 0, own_dot, jnp.where(row == 1, curvature, 0.0)
    )
    send_all(3, lambda peer: sums_out, sums_in)
    wait_all(recv_sem, 3, sums_in)
    sums = jnp.sum(sums_in[:, corners:, :], axis=0)
    precond_dot = sums[0:1]
    step = precond_dot / sums[1:2]
    solve_corners(picked - step * sums_in[:, :corners, :].reshape(n * corners, lanes))

    def update_tile(index, carry):
        s, _, at = tile(index)
        value = res[s, at, :] - step * app[s, at, :]
        res[s, at, :] = value
        weighted[s, at, :] = (weight[s, at, :] * value).astype(jnp.bfloat16)
        return carry

    lax.fori_loop(0, tiles, update_tile, 0)

    def second_tile(index, acc):
        s, _, at = tile(index)
        value = weight[s, at, :] * product(index, weighted) + corner_tile(s, at)
        app[s, at, :] = value
        return acc + fold(value * res[s, at, :])

    dots_out[0] = lax.fori_loop(0, tiles, second_tile, zero)
    send_all(4, lambda peer: dots_out.at[0], dots_in.at[0])
    out[...] = step[None] * dirn[...]
    wait_all(recv_sem, 4, dots_in.at[0])
    next_dot = jnp.sum(jnp.sum(dots_in[0], axis=0), axis=0, keepdims=True)
    ratio = next_dot / precond_dot
    for k in reversed(range(FACES)):
        at = pl.ds(k * FW, FW)
        for s in range(SUB_DEV):
            value = app[s, at, :] + ratio * dirn[s, at, :]
            dirn[s, at, :] = value
            rounded[1, s, at, :] = value.astype(jnp.bfloat16)
        face_copy(1, k).start()
    dots_out[1] = apply(1)
    send_all(5, lambda peer: dots_out.at[1], dots_in.at[1])
    wait_all(recv_sem, 5, dots_in.at[1])
    step = next_dot / jnp.sum(jnp.sum(dots_in[1], axis=0), axis=0, keepdims=True)
    out[...] = out[...] + step[None] * dirn[...]

    for turn in range(2):
        for k in range(FACES):
            face_copy(turn, k).wait_send()
    landed = [loads_in, common_in, picks_in, sums_in, dots_in.at[0], dots_in.at[1]]
    for which, target in enumerate(landed):
        wait_all(send_sem, which, target)


def on_device(
    schur_block,
    scaling,
    gravity_load,
    pressure,
    block_target,
    aero_interp,
    partner_slot,
    corner_row,
    corner_coarse,
    coarse_inverse,
):
    n = lax.axis_size("sub")
    columns = gravity_load.shape[2]
    count, points, _ = pressure.shape
    size = gravity_load.shape[1]
    corners = corner_row.size
    key = (block_target * points + jnp.arange(points)[None, :]).reshape(-1)
    chosen = jnp.arange(SUB_DEV * n * points)[:, None] == key[None, :]
    loads = jnp.dot(
        chosen.astype(jnp.bfloat16),
        pressure.reshape(count * points, columns),
        preferred_element_type=jnp.float32,
    ).reshape(n, SUB_DEV * points, columns)
    names = jnp.broadcast_to(
        corner_coarse.reshape(corners, 1).astype(jnp.float32), (corners, columns)
    )
    inverse = coarse_inverse.reshape(coarse_inverse.shape[0], -1, columns)
    inverse = jnp.swapaxes(inverse, 0, 1).reshape(-1, columns)
    common = jnp.concatenate([names, inverse], axis=0)
    interp = (
        jnp.eye(SUB_DEV, dtype=jnp.float32)[:, None, :, None] * aero_interp.T[None, :, None, :]
    ).reshape(SUB_DEV, size, SUB_DEV * points)
    spread = (corner_row[:, None, :] == jnp.arange(size)[None, :, None]).astype(jnp.bfloat16)
    spread = jnp.concatenate([spread] * 3 + [jnp.zeros_like(spread)], axis=2)
    weight = jnp.broadcast_to(scaling[:, :, None], gravity_load.shape)
    per_sub = corner_row.shape[1]
    vmem = pl.BlockSpec(memory_space=pltpu.VMEM)
    smem = pl.BlockSpec(memory_space=pltpu.SMEM)
    f32, bf16 = jnp.float32, jnp.bfloat16
    field = (SUB_DEV, size, columns)
    return pl.pallas_call(
        functools.partial(kernel, n, coarse_inverse.shape[1] // columns),
        out_shape=jax.ShapeDtypeStruct(field, f32),
        in_specs=[pl.BlockSpec(memory_space=pl.ANY)] + [vmem] * 6 + [smem] * 2,
        out_specs=vmem,
        scratch_shapes=[
            pltpu.VMEM((2,) + schur_block.shape, bf16),
            pltpu.VMEM(field, f32),
            pltpu.VMEM(field, f32),
            pltpu.VMEM(field, f32),
            pltpu.VMEM(field, bf16),
            pltpu.VMEM((2,) + field, bf16),
            pltpu.VMEM((SUB_DEV, 4 * per_sub, columns), bf16),
            pltpu.VMEM((corners, n * corners), f32),
            pltpu.VMEM((2, FACES, SUB_DEV, FW, columns), bf16),
            pltpu.VMEM((corners, columns), f32),
            pltpu.VMEM((corners + 8, columns), f32),
            pltpu.VMEM((2, 8, columns), f32),
            pltpu.VMEM(loads.shape, f32),
            pltpu.VMEM((n,) + common.shape, f32),
            pltpu.VMEM((n, corners, columns), f32),
            pltpu.VMEM((n, corners + 8, columns), f32),
            pltpu.VMEM((2, n, 8, columns), f32),
            pltpu.SemaphoreType.DMA((3,)),
            pltpu.SemaphoreType.DMA((2, FACES)),
            pltpu.SemaphoreType.DMA((2, FACES)),
            pltpu.SemaphoreType.DMA((6,)),
            pltpu.SemaphoreType.DMA((6,)),
        ],
        compiler_params=pltpu.CompilerParams(
            collective_id=0, has_side_effects=True, vmem_limit_bytes=44 << 20
        ),
    )(schur_block, weight, gravity_load, loads, common, interp, spread, partner_slot, corner_row)


def solution(mesh):
    return jax.shard_map(
        on_device,
        mesh=mesh,
        in_specs=(
            P("sub", "rhs", None),
            P("sub", None),
            P("sub", None, "rhs"),
            P("sub", None, "rhs"),
            P("sub", None),
            P(),
            P(None, "sub"),
            P("sub", None),
            P("sub", None),
            P("sub", None),
        ),
        out_specs=P("sub", None, "rhs"),
        check_vma=False,
    )
```

time: 577 us -> 60.4 us (0.10)
  blocking collectives: 211 us -> 0 us
  waiting for transfers between devices: 206 us -> 0 us
  local copies, waits for them, and re-layouts: 71.8 us -> 5.35 us
  Pallas kernels: 0 us -> 51.2 us
  other arithmetic: 33.9 us -> 3.23 us
  matrix products: 23 us -> 0.2 us
  between operations: 15.4 us -> 0.11 us
  starting transfers between devices: 13.9 us -> 0 us
    psum x2 -> x0, waiting for transfers between devices: 196 us -> none  [precondition(): coarse = lax.psum(partial_sum, 'sub')]
    psum x3 -> x0, blocking collectives: 115 us -> none  [the longest x2 76.4 us: precondition(): product_value = lax.psum(jnp.sum(residual * precond, axis=(0, 1)), 'sub')]
    all_gather x2 -> x0, blocking collectives: 78.2 us -> none  [coarse_solve(): return lax.all_gather(own_rows, 'sub', axis=0, tiled=True)]
    pallas_call x0 -> x1, Pallas kernels: none -> 51.2 us  [on_device(): pl.pallas_call(functools.partial(kernel, n, coarse_inverse.shape[1] // co...]
    dot_general x15 -> x1, matrix products: 23 us -> 0.2 us  [on_device(): jnp.dot(chosen.astype(jnp.bfloat16), pressure.reshape(count * points, col...]
    all_to_all x8 -> x0, local copies, waits for them, and re-layouts: 18.7 us -> none  [schur_apply(): lax.all_to_all(half_rows, 'rhs', split_axis=2, concat_axis=1, tiled=True)]
    all_to_all x4 -> x0, blocking collectives: 18.3 us -> none  [schur_apply(): lax.all_to_all(half_rows, 'rhs', split_axis=2, concat_axis=1, tiled=True)]
    dot_general x12 -> x0, local copies, waits for them, and re-layouts: 10.1 us -> none  [the longest x8 6.84 us: jump_terms(): jnp.einsum('sj,jfc->sfc', select, partner_face, preferred_element_type=jn...]
  transfers between devices with their start and end apart: 15 -> 0, of which waited for: 6 -> 0; matrix products, arithmetic and copies ran while one was open for 7% -> 0% of each run, Pallas kernels for 0% -> 0%
where the time goes in v2:
time: 60.4 us; the launch traced here: 60.1 us
  Pallas kernels  51.2 us (85%)
  local copies, waits for them, and re-layouts  5.35 us (9%)
  other arithmetic  3.23 us (5%)
    pallas_call x1, Pallas kernels, on_device(): pl.pallas_call(functools.partial(kernel, n, coarse_inverse.shape[1] // co...  51.2 us
    unnamed x12, local copies, waits for them, and re-layouts  3.37 us

profile of v2, /device:TPU:0, one launch (start us, length us, event | category | flops | bytes accessed | tf_op | source)
XLA Modules:
  0.0 60.1 jit_solution(817095078851265773)
XLA Ops:
  0.0 0.0 copy-start
  0.0 0.0 copy-start.4
  0.0 0.8 %copy-done = bf16[64,4,128]{2,1,0:T(4,128)(2,1)S(1)} copy-done((bf16[64,4,128]{2,1,0:T(4,128)(2,1)S(1)}, bf16[64,4,128]{2,1,0:T(4,128)(2,1)}, u32[]{:S(2)}) %copy-start) | copy-done | bytes 65560
  0.8 0.7 %multiply_bitcast_fusion = s32[64]{0:T(128)S(1)} fusion(s32[64,1]{0,1:T(1,128)} %param.14), kind=kLoop, calls=%fused_computation.12 | loop fusion | flops 64 | bytes 512 | tf_op jit(solution)/shard_map/add | solution.py:317
  1.5 0.1 pad.3.clone
  1.6 0.7 %convert_element_type.22 = f32[2,8]{1,0:T(2,128)S(1)} convert(s32[2,8]{1,0:T(2,128)} %param.18) | non-fusion elementwise | flops 16 | bytes 128 | tf_op jit(solution)/shard_map/convert_element_type | solution.py:325
  2.3 0.1 reshape.61
  2.4 0.1 mul.30
  2.4 0.1 mul.31
  2.5 0.8 %copy.17.slots = s32[4,2]{1,0:T(4,128)S(1)} copy(s32[4,2]{0,1:T(2,128)} %param.16) | data formatting | bytes 64 | tf_op args[6]
  3.3 0.8 %pad_maximum_fusion.common = f32[24,128]{1,0:T(8,128)S(1)} fusion(f32[8,128]{1,0:T(8,128)} %param.19, f32[24]{0:T(128)S(1)} %pad.4.clone), kind=kLoop, calls=%fused_computation.9 | loop fusion | flops 3072 | bytes 16480 | tf_op jit(solution)/shard_map/concatenate | solution.py:329
  4.0 0.1 iota_add_fusion
  4.1 0.1 add.30
  4.2 0.7 %mul.33 = f32[1024,2,4]{0,2,1:T(4,128)S(1)} broadcast(f32[1024,4]{0,1:T(4,128)} %bitcast.10), dimensions={0,2} | broadcast | bytes 49152 | tf_op jit(solution)/shard_map/mul | solution.py:331
  5.0 0.0 copy-start.1
  5.0 0.0 copy-start.3
  5.0 0.9 %fusion.4 = bf16[2,1024,8]{1,2,0:T(8,128)(2,1)S(1)} fusion(s32[2,8]{1,0:T(2,128)} %corner_row.1), kind=kLoop, calls=%fused_computation.7 | loop fusion | flops 32768 | bytes 32832 | tf_op jit(solution)/shard_map/convert_element_type | solution.py:333
  5.9 0.2 fusion.loads
  6.1 0.1 maximum_maximum_fusion
  6.2 0.3 copy.16.spread
  6.5 0.2 copy.15
  6.7 0.0 copy-start.2
  6.7 0.1 broadcast_multiply_fusion.interp
  6.8 0.0 copy-done.4
  6.8 0.3 broadcast_in_dim.6.weight
  7.1 0.0 copy-done.1
  7.1 0.0 copy-done.3
  7.1 0.8 %copy-done.2 = f32[2,1024,128]{2,1,0:T(8,128)S(1)} copy-done((f32[2,1024,128]{2,1,0:T(8,128)S(1)}, f32[2,1024,128]{2,1,0:T(8,128)}, u32[]{:S(2)}) %copy-start.2) | copy-done | bytes 1048600
  7.9 51.2 %shard_map.100 = f32[2,1024,128]{2,1,0:T(8,128)S(1)} custom-call(bf16[2,512,1024]{2,1,0:T(8,128)(2,1)S(1)} %copy-done.1, f32[2,1024,128]{2,1,0:T(8,128)S(1)} %broadcast_in_dim.6.weight, f32[2,1024,128]{2,1,0:T(8,128)S(1)} %copy-done.2, f32[16,8,128]{2,1,0:T(8,128)S(1)} %fusion.loads, f32[24,128]{1,0:T(8,128)S(1)} %pad_maximum_fusion.common, ...), custom_call_target="tpu_custom_call" | custom-call | tf_op jit(solution)/shard_map/pallas_call | solution.py:341
  59.1 1.0 %copy.19 = f32[2,1024,128]{2,1,0:T(8,128)} copy(f32[2,1024,128]{2,1,0:T(8,128)S(1)} %shard_map.100) | data formatting | bytes 2097152
  (5 shorter events, 0.0 us)
Async XLA Ops:
  0.0 0.8 %copy-start = (bf16[64,4,128]{2,1,0:T(4,128)(2,1)S(1)}, bf16[64,4,128]{2,1,0:T(4,128)(2,1)}, u32[]{:S(2)}) copy-start(bf16[64,4,128]{2,1,0:T(4,128)(2,1)} %param.13) | copy-start | bytes 196612
  0.0 6.8 %copy-start.4 = (f32[2,1024]{1,0:T(2,128)S(1)}, f32[2,1024]{1,0:T(2,128)}, u32[]{:S(2)}) copy-start(f32[2,1024]{1,0:T(2,128)} %param.11) | copy-start | bytes 24580
  5.0 2.1 %copy-start.1 = (bf16[2,512,1024]{2,1,0:T(8,128)(2,1)S(1)}, bf16[2,512,1024]{2,1,0:T(8,128)(2,1)}, u32[]{:S(2)}) copy-start(bf16[2,512,1024]{2,1,0:T(8,128)(2,1)} %schur.1) | copy-start | bytes 6291460
  5.0 2.1 %copy-start.3 = (s32[2,8]{1,0:T(2,128)S(1)}, s32[2,8]{1,0:T(2,128)}, u32[]{:S(2)}) copy-start(s32[2,8]{1,0:T(2,128)} %corner_row.1) | copy-start | bytes 196
  6.7 1.2 %copy-start.2 = (f32[2,1024,128]{2,1,0:T(8,128)S(1)}, f32[2,1024,128]{2,1,0:T(8,128)}, u32[]{:S(2)}) copy-start(f32[2,1024,128]{2,1,0:T(8,128)} %gravity.1) | copy-start | bytes 3145732

commit v3 on v2

--- a/solution.py
+++ b/solution.py
@@ -24,15 +24,19 @@
     n,
     chunks,
     schur,
+    scaling,
+    gravity,
+    pressure,
+    key,
+    inverse,
+    interp,
+    slots,
+    corner_row,
+    corner_coarse,
+    out,
     weight,
-    gravity,
     loads,
     common,
-    interp,
-    spread,
-    slots,
-    corner_row,
-    out,
     matrix,
     res,
     dirn,
@@ -61,9 +65,8 @@
     rows = schur.shape[1]
     corners = corner_row.shape[0] * corner_row.shape[1]
     per_sub = corner_row.shape[1]
-    coarse_rows = common.shape[0] - corners
-    blocks = gravity.shape[1] // FW
-    half_blocks = rows // FW
+    halves = gravity.shape[1] // rows
+    lanes = common.shape[1]
 
     local = pltpu.make_async_copy(schur, matrix.at[half], matrix_sem.at[0])
     local.start()
@@ -78,6 +81,30 @@
 
     lax.fori_loop(1, n, greet, 0)
     pl.semaphore_signal(barrier, inc=1, device_id={"rhs": 1 - half}, device_id_type=MESH)
+
+    for s in range(SUB_DEV):
+        for k in range(FACES):
+            at = slice(k * FW, (k + 1) * FW)
+            weight[s, at, :] = jnp.broadcast_to(scaling[s : s + 1, at], (lanes, FW)).T
+        for i in range(per_sub):
+            name = corner_coarse[s, i].astype(jnp.float32)
+            common[pl.ds(s * per_sub + i, 1), :] = jnp.full((1, lanes), name, jnp.float32)
+    per_device = inverse.shape[0]
+    for c in range(chunks):
+        common[pl.ds(corners + c * per_device, per_device), :] = inverse[
+            :, c * lanes : (c + 1) * lanes
+        ]
+    width = loads.shape[1]
+    group = 128 // width
+
+    def sum_loads(index, carry):
+        row = index * 128 + lax.broadcasted_iota(jnp.int32, (128, key.shape[1]), 0)
+        chosen = jnp.where(row == key[...], 1.0, 0.0).astype(jnp.bfloat16)
+        total = jnp.dot(chosen, pressure[...], preferred_element_type=jnp.float32)
+        loads[pl.ds(index * group, group)] = total.reshape(group, width, lanes)
+        return carry
+
+    lax.fori_loop(0, n // group, sum_loads, 0)
     pl.semaphore_wait(barrier, n)
 
     def send_all(which, source, target):
@@ -113,18 +140,15 @@
     swap.start()
 
     def tile(index):
-        s, k = index // blocks, lax.rem(index, blocks)
-        return s, k, pl.ds(pl.multiple_of(k * FW, FW), FW)
+        s, part = index // halves, lax.rem(index, halves)
+        return s, part, pl.ds(pl.multiple_of(part * rows, rows), rows)
 
     def product(index, vector):
-        s, k, _ = tile(index)
-        part = pl.ds(pl.multiple_of(lax.rem(k, half_blocks) * FW, FW), FW)
-        return jnp.dot(
-            matrix[k // half_blocks, s, part, :], vector[s], preferred_element_type=jnp.float32
-        )
+        s, part, _ = tile(index)
+        return jnp.dot(matrix[part, s], vector[s], preferred_element_type=jnp.float32)
 
     zero = jnp.zeros((8, out.shape[2]), jnp.float32)
-    tiles = SUB_DEV * blocks
+    tiles = SUB_DEV * halves
 
     def face_copy(turn, k):
         bit = 1 << k
@@ -154,16 +178,33 @@
             stack = [high[at], middle[at], low[at], jnp.zeros_like(low[at])]
             corner[s] = jnp.concatenate(stack, axis=0).astype(jnp.bfloat16)
 
-    def corner_tile(s, at):
-        return jnp.dot(spread[s, at, :], corner[s], preferred_element_type=jnp.float32)
+    places = []
+    column = lax.broadcasted_iota(jnp.int32, (1, 4 * per_sub), 1)
+    for s in range(SUB_DEV):
+        place = jnp.full_like(column, -1)
+        for i in range(per_sub):
+            mine = (lax.rem(column, per_sub) == i) & (column < 3 * per_sub)
+            place = jnp.where(mine, corner_row[s, i], place)
+        places.append(place)
+
+    def corner_tile(s, first, size):
+        row = first + lax.broadcasted_iota(jnp.int32, (size, 4 * per_sub), 0)
+        place = places[s] if isinstance(s, int) else jnp.where(s == 0, places[0], places[1])
+        spread = jnp.where(row == place, 1.0, 0.0).astype(jnp.bfloat16)
+        return jnp.dot(spread, corner[s], preferred_element_type=jnp.float32)
 
     wait_all(recv_sem, 0, loads_in)
     load_sum = jnp.sum(loads_in[...], axis=0)
 
     def start_tile(index, carry):
         s, _, at = tile(index)
-        force = gravity[s, at, :] + jnp.dot(
-            interp[s, at, :], load_sum, precision=EXACT, preferred_element_type=jnp.float32
+        mine = jnp.where(s == 0, load_sum[: width // 2], load_sum[width // 2 :])
+        force = gravity[s, at, :] + lax.dot_general(
+            interp[:, at],
+            mine,
+            (((0,), (0,)), ((), ())),
+            precision=EXACT,
+            preferred_element_type=jnp.float32,
         )
         res[s, at, :] = force
         weighted[s, at, :] = (weight[s, at, :] * force).astype(jnp.bfloat16)
@@ -174,8 +215,6 @@
     send_all(2, lambda peer: picks_out, picks_in)
 
     wait_all(recv_sem, 1, common_in)
-    lanes = common.shape[1]
-    per_device = coarse_rows // chunks
     lane = lax.broadcasted_iota(jnp.int32, (1, lanes), 1).astype(jnp.float32)
 
     def one_hot(names, chunk):
@@ -214,7 +253,7 @@
     for k in reversed(range(FACES)):
         at = pl.ds(k * FW, FW)
         for s in range(SUB_DEV):
-            value = dirn[s, at, :] + corner_tile(s, at)
+            value = dirn[s, at, :] + corner_tile(s, k * FW, FW)
             dirn[s, at, :] = value
             rounded[0, s, at, :] = value.astype(jnp.bfloat16)
             acc += fold(value * res[s, at, :])
@@ -234,7 +273,7 @@
             face_copy(turn, k).wait_recv()
             at = pl.ds(k * FW, FW)
             for s in range(SUB_DEV):
-                far = jnp.where(slots[k, s] == 0, faces[turn, k, 0], faces[turn, k, 1])
+                far = jnp.where(slots[s, k] == 0, faces[turn, k, 0], faces[turn, k, 1])
                 far = far.astype(jnp.float32)
                 value = app[s, at, :] - COUPLING * far
                 if turn == 0:
@@ -265,8 +304,8 @@
     lax.fori_loop(0, tiles, update_tile, 0)
 
     def second_tile(index, acc):
-        s, _, at = tile(index)
-        value = weight[s, at, :] * product(index, weighted) + corner_tile(s, at)
+        s, part, at = tile(index)
+        value = weight[s, at, :] * product(index, weighted) + corner_tile(s, part * rows, rows)
         app[s, at, :] = value
         return acc + fold(value * res[s, at, :])
 
@@ -314,36 +353,22 @@
     count, points, _ = pressure.shape
     size = gravity_load.shape[1]
     corners = corner_row.size
-    key = (block_target * points + jnp.arange(points)[None, :]).reshape(-1)
-    chosen = jnp.arange(SUB_DEV * n * points)[:, None] == key[None, :]
-    loads = jnp.dot(
-        chosen.astype(jnp.bfloat16),
-        pressure.reshape(count * points, columns),
-        preferred_element_type=jnp.float32,
-    ).reshape(n, SUB_DEV * points, columns)
-    names = jnp.broadcast_to(
-        corner_coarse.reshape(corners, 1).astype(jnp.float32), (corners, columns)
-    )
-    inverse = coarse_inverse.reshape(coarse_inverse.shape[0], -1, columns)
-    inverse = jnp.swapaxes(inverse, 0, 1).reshape(-1, columns)
-    common = jnp.concatenate([names, inverse], axis=0)
-    interp = (
-        jnp.eye(SUB_DEV, dtype=jnp.float32)[:, None, :, None] * aero_interp.T[None, :, None, :]
-    ).reshape(SUB_DEV, size, SUB_DEV * points)
-    spread = (corner_row[:, None, :] == jnp.arange(size)[None, :, None]).astype(jnp.bfloat16)
-    spread = jnp.concatenate([spread] * 3 + [jnp.zeros_like(spread)], axis=2)
-    weight = jnp.broadcast_to(scaling[:, :, None], gravity_load.shape)
+    key = (block_target * points + jnp.arange(points)[None, :]).reshape(1, -1)
     per_sub = corner_row.shape[1]
     vmem = pl.BlockSpec(memory_space=pltpu.VMEM)
     smem = pl.BlockSpec(memory_space=pltpu.SMEM)
     f32, bf16 = jnp.float32, jnp.bfloat16
     field = (SUB_DEV, size, columns)
+    common = (corners + coarse_inverse.size // columns, columns)
     return pl.pallas_call(
         functools.partial(kernel, n, coarse_inverse.shape[1] // columns),
         out_shape=jax.ShapeDtypeStruct(field, f32),
-        in_specs=[pl.BlockSpec(memory_space=pl.ANY)] + [vmem] * 6 + [smem] * 2,
+        in_specs=[pl.BlockSpec(memory_space=pl.ANY)] + [vmem] * 6 + [smem] * 3,
         out_specs=vmem,
         scratch_shapes=[
+            pltpu.VMEM(field, f32),
+            pltpu.VMEM((n, SUB_DEV * points, columns), f32),
+            pltpu.VMEM(common, f32),
             pltpu.VMEM((2,) + schur_block.shape, bf16),
             pltpu.VMEM(field, f32),
             pltpu.VMEM(field, f32),
@@ -356,8 +381,8 @@
             pltpu.VMEM((corners, columns), f32),
             pltpu.VMEM((corners + 8, columns), f32),
             pltpu.VMEM((2, 8, columns), f32),
-            pltpu.VMEM(loads.shape, f32),
-            pltpu.VMEM((n,) + common.shape, f32),
+            pltpu.VMEM((n, SUB_DEV * points, columns), f32),
+            pltpu.VMEM((n,) + common, f32),
             pltpu.VMEM((n, corners, columns), f32),
             pltpu.VMEM((n, corners + 8, columns), f32),
             pltpu.VMEM((2, n, 8, columns), f32),
@@ -370,7 +395,18 @@
         compiler_params=pltpu.CompilerParams(
             collective_id=0, has_side_effects=True, vmem_limit_bytes=44 << 20
         ),
-    )(schur_block, weight, gravity_load, loads, common, interp, spread, partner_slot, corner_row)
+    )(
+        schur_block,
+        scaling,
+        gravity_load,
+        pressure.reshape(count * points, columns),
+        key,
+        coarse_inverse,
+        aero_interp,
+        partner_slot.T,
+        corner_row,
+        corner_coarse,
+    )
 
 
 def solution(mesh):

time: 60.4 us -> 60.5 us (level)
  local copies, waits for them, and re-layouts: 5.35 us -> 8.87 us
  other arithmetic: 3.23 us -> 0.73 us
  Pallas kernels: 51.2 us -> 50.5 us
    unnamed x12 -> x19, local copies, waits for them, and re-layouts: 3.37 us -> 8.76 us
    convert_element_type x3 -> x0, other arithmetic: 1.59 us -> none  [the longest x1 0.9 us: on_device(): (corner_row[:, None, :] == jnp.arange(size)[None, :, None]).astype(jnp.bf...]
    mul x5 -> x0, local copies, waits for them, and re-layouts: 1.1 us -> none  [on_device(): jnp.eye(SUB_DEV, dtype=jnp.float32)[:, None, :, None]]
    concatenate x2 -> x0, other arithmetic: 0.84 us -> none  [the longest x1 0.76 us: on_device(): common = jnp.concatenate([names, inverse], axis=0)]
    pallas_call x1, Pallas kernels: 51.2 us -> 50.5 us  [on_device(): pl.pallas_call(functools.partial(kernel, n, coarse_inverse.shape[1] // co...]
where the time goes in v3:
time: 60.5 us; the launch traced here: 60.1 us
  Pallas kernels  50.5 us (83%)
  local copies, waits for them, and re-layouts  8.87 us (15%)
  other arithmetic  0.73 us (1%)
    pallas_call x1, Pallas kernels, on_device(): pl.pallas_call(functools.partial(kernel, n, coarse_inverse.shape[1] // co...  50.5 us
    unnamed x19, local copies, waits for them, and re-layouts  8.76 us

profile of v3, /device:TPU:0, one launch (start us, length us, event | category | flops | bytes accessed | tf_op | source)
XLA Modules:
  0.0 60.1 jit_solution(2308322549797286335)
XLA Ops:
  0.0 0.7 %multiply_bitcast_fusion = s32[64]{0:T(128)S(1)} fusion(s32[64,1]{0,1:T(1,128)} %param.14), kind=kLoop, calls=%fused_computation.1 | loop fusion | flops 64 | bytes 512 | tf_op jit(solution)/shard_map/add | solution.py:356
  0.7 0.1 iota_add_fusion
  0.7 0.1 add.29.key
  0.8 0.0 copy-start
  0.9 1.6 %copy-done = bf16[2,512,1024]{2,1,0:T(8,128)(2,1)S(1)} copy-done((bf16[2,512,1024]{2,1,0:T(8,128)(2,1)S(1)}, bf16[2,512,1024]{2,1,0:T(8,128)(2,1)}, u32[]{:S(2)}) %copy-start) | copy-done | bytes 2097176
  2.4 0.0 copy-start.1
  2.4 1.2 %copy-done.1 = f32[2,1024,128]{2,1,0:T(8,128)S(1)} copy-done((f32[2,1024,128]{2,1,0:T(8,128)S(1)}, f32[2,1024,128]{2,1,0:T(8,128)}, u32[]{:S(2)}) %copy-start.1) | copy-done | bytes 1048600
  3.7 0.0 copy-start.2
  3.7 0.8 %copy-done.2 = bf16[64,4,128]{2,1,0:T(4,128)(2,1)S(1)} copy-done((bf16[64,4,128]{2,1,0:T(4,128)(2,1)S(1)}, bf16[64,4,128]{2,1,0:T(4,128)(2,1)}, u32[]{:S(2)}) %copy-start.2) | copy-done | bytes 65560
  4.5 0.0 copy-start.3
  4.5 0.7 %copy-done.3 = f32[4,1024]{1,0:T(4,128)S(1)} copy-done((f32[4,1024]{1,0:T(4,128)S(1)}, f32[4,1024]{1,0:T(4,128)}, u32[]{:S(2)}) %copy-start.3) | copy-done | bytes 16408
  5.2 0.0 copy-start.4
  5.2 0.7 %copy-done.4 = f32[2,1024]{1,0:T(2,128)S(1)} copy-done((f32[2,1024]{1,0:T(2,128)S(1)}, f32[2,1024]{1,0:T(2,128)}, u32[]{:S(2)}) %copy-start.4) | copy-done | bytes 8216
  5.9 0.0 copy-start.5
  5.9 0.7 %copy-done.5 = f32[8,128]{1,0:T(8,128)S(1)} copy-done((f32[8,128]{1,0:T(8,128)S(1)}, f32[8,128]{1,0:T(8,128)}, u32[]{:S(2)}) %copy-start.5) | copy-done | bytes 4120
  6.6 0.0 copy-start.6
  6.6 0.7 %copy-done.6 = s32[4,2]{0,1:T(2,128)S(1)} copy-done((s32[4,2]{0,1:T(2,128)S(1)}, s32[4,2]{0,1:T(2,128)}, u32[]{:S(2)}) %copy-start.6) | copy-done | bytes 56
  7.3 0.0 copy-start.7
  7.3 0.7 %copy-done.7 = s32[2,8]{1,0:T(2,128)S(1)} copy-done((s32[2,8]{1,0:T(2,128)S(1)}, s32[2,8]{1,0:T(2,128)}, u32[]{:S(2)}) %copy-start.7) | copy-done | bytes 88
  8.0 0.0 copy-start.8
  8.0 0.7 %copy-done.8 = s32[2,8]{1,0:T(2,128)S(1)} copy-done((s32[2,8]{1,0:T(2,128)S(1)}, s32[2,8]{1,0:T(2,128)}, u32[]{:S(2)}) %copy-start.8) | copy-done | bytes 88
  8.6 50.5 %shard_map.100 = f32[2,1024,128]{2,1,0:T(8,128)S(1)} custom-call(bf16[2,512,1024]{2,1,0:T(8,128)(2,1)S(1)} %copy-done, f32[2,1024]{1,0:T(2,128)S(1)} %copy-done.4, f32[2,1024,128]{2,1,0:T(8,128)S(1)} %copy-done.1, bf16[256,128]{1,0:T(8,128)(2,1)S(1)} %bitcast.4, s32[1,256]{1,0:T(1,128)S(1)} %add.29.key, f32[8,128]{1,0:T(8,128)S(1)} %copy-done.5, ...), custom_call_target="tpu_custom_call" | custom-call | tf_op jit(solution)/shard_map/pallas_call | solution.py:363
  59.2 1.0 %copy.12 = f32[2,1024,128]{2,1,0:T(8,128)} copy(f32[2,1024,128]{2,1,0:T(8,128)S(1)} %shard_map.100) | data formatting | bytes 2097152
Async XLA Ops:
  0.8 1.6 %copy-start = (bf16[2,512,1024]{2,1,0:T(8,128)(2,1)S(1)}, bf16[2,512,1024]{2,1,0:T(8,128)(2,1)}, u32[]{:S(2)}) copy-start(bf16[2,512,1024]{2,1,0:T(8,128)(2,1)} %schur.1) | copy-start | bytes 6291460
  2.4 1.2 %copy-start.1 = (f32[2,1024,128]{2,1,0:T(8,128)S(1)}, f32[2,1024,128]{2,1,0:T(8,128)}, u32[]{:S(2)}) copy-start(f32[2,1024,128]{2,1,0:T(8,128)} %gravity.1) | copy-start | bytes 3145732
  3.7 0.8 %copy-start.2 = (bf16[64,4,128]{2,1,0:T(4,128)(2,1)S(1)}, bf16[64,4,128]{2,1,0:T(4,128)(2,1)}, u32[]{:S(2)}) copy-start(bf16[64,4,128]{2,1,0:T(4,128)(2,1)} %param.13) | copy-start | bytes 196612
  4.5 0.7 %copy-start.3 = (f32[4,1024]{1,0:T(4,128)S(1)}, f32[4,1024]{1,0:T(4,128)}, u32[]{:S(2)}) copy-start(f32[4,1024]{1,0:T(4,128)} %interp.1) | copy-start | bytes 49156
  5.2 0.7 %copy-start.4 = (f32[2,1024]{1,0:T(2,128)S(1)}, f32[2,1024]{1,0:T(2,128)}, u32[]{:S(2)}) copy-start(f32[2,1024]{1,0:T(2,128)} %scaling.1) | copy-start | bytes 24580
  5.9 0.7 %copy-start.5 = (f32[8,128]{1,0:T(8,128)S(1)}, f32[8,128]{1,0:T(8,128)}, u32[]{:S(2)}) copy-start(f32[8,128]{1,0:T(8,128)} %inverse.1) | copy-start | bytes 12292
  6.6 0.7 %copy-start.6 = (s32[4,2]{0,1:T(2,128)S(1)}, s32[4,2]{0,1:T(2,128)}, u32[]{:S(2)}) copy-start(s32[4,2]{0,1:T(2,128)} %param.16) | copy-start | bytes 100
  7.3 0.7 %copy-start.7 = (s32[2,8]{1,0:T(2,128)S(1)}, s32[2,8]{1,0:T(2,128)}, u32[]{:S(2)}) copy-start(s32[2,8]{1,0:T(2,128)} %corner_row.1) | copy-start | bytes 196
  8.0 0.7 %copy-start.8 = (s32[2,8]{1,0:T(2,128)S(1)}, s32[2,8]{1,0:T(2,128)}, u32[]{:S(2)}) copy-start(s32[2,8]{1,0:T(2,128)} %corner_coarse.1) | copy-start | bytes 196

commit v4 on v3

--- a/solution.py
+++ b/solution.py
@@ -24,16 +24,20 @@
     n,
     chunks,
     schur,
+    scaling_far,
+    gravity_far,
+    pressure_far,
+    key_far,
+    inverse_far,
+    interp_far,
+    indices,
+    out,
     scaling,
-    gravity,
     pressure,
     key,
     inverse,
     interp,
-    slots,
-    corner_row,
-    corner_coarse,
-    out,
+    load_sem,
     weight,
     loads,
     common,
@@ -63,13 +67,24 @@
     me = lax.axis_index("sub")
     half = lax.axis_index("rhs")
     rows = schur.shape[1]
-    corners = corner_row.shape[0] * corner_row.shape[1]
-    per_sub = corner_row.shape[1]
-    halves = gravity.shape[1] // rows
+    per_sub = (indices.shape[1] - FACES) // 2
+    corners = SUB_DEV * per_sub
+    halves = res.shape[1] // rows
     lanes = common.shape[1]
 
     local = pltpu.make_async_copy(schur, matrix.at[half], matrix_sem.at[0])
     local.start()
+    fetches = []
+    for source, target in [
+        (scaling_far, scaling),
+        (inverse_far, inverse),
+        (key_far, key),
+        (pressure_far, pressure),
+        (interp_far, interp),
+        (gravity_far, res),
+    ]:
+        fetches.append(pltpu.make_async_copy(source, target, load_sem.at[len(fetches)]))
+        fetches[-1].start()
 
     barrier = pltpu.get_barrier_semaphore()
 
@@ -82,12 +97,14 @@
     lax.fori_loop(1, n, greet, 0)
     pl.semaphore_signal(barrier, inc=1, device_id={"rhs": 1 - half}, device_id_type=MESH)
 
+    for fetch in fetches:
+        fetch.wait()
     for s in range(SUB_DEV):
         for k in range(FACES):
             at = slice(k * FW, (k + 1) * FW)
             weight[s, at, :] = jnp.broadcast_to(scaling[s : s + 1, at], (lanes, FW)).T
         for i in range(per_sub):
-            name = corner_coarse[s, i].astype(jnp.float32)
+            name = indices[s, FACES + per_sub + i].astype(jnp.float32)
             common[pl.ds(s * per_sub + i, 1), :] = jnp.full((1, lanes), name, jnp.float32)
     per_device = inverse.shape[0]
     for c in range(chunks):
@@ -165,7 +182,7 @@
     def pick(source, target):
         for s in range(SUB_DEV):
             for i in range(per_sub):
-                target[pl.ds(s * per_sub + i, 1), :] = source[s, pl.ds(corner_row[s, i], 1), :]
+                target[pl.ds(s * per_sub + i, 1), :] = source[s, pl.ds(indices[s, FACES + i], 1), :]
 
     def solve_corners(picked):
         solved = jnp.dot(mix[...], picked, precision=EXACT, preferred_element_type=jnp.float32)
@@ -184,7 +201,7 @@
         place = jnp.full_like(column, -1)
         for i in range(per_sub):
             mine = (lax.rem(column, per_sub) == i) & (column < 3 * per_sub)
-            place = jnp.where(mine, corner_row[s, i], place)
+            place = jnp.where(mine, indices[s, FACES + i], place)
         places.append(place)
 
     def corner_tile(s, first, size):
@@ -199,7 +216,7 @@
     def start_tile(index, carry):
         s, _, at = tile(index)
         mine = jnp.where(s == 0, load_sum[: width // 2], load_sum[width // 2 :])
-        force = gravity[s, at, :] + lax.dot_general(
+        force = res[s, at, :] + lax.dot_general(
             interp[:, at],
             mine,
             (((0,), (0,)), ((), ())),
@@ -273,7 +290,7 @@
             face_copy(turn, k).wait_recv()
             at = pl.ds(k * FW, FW)
             for s in range(SUB_DEV):
-                far = jnp.where(slots[s, k] == 0, faces[turn, k, 0], faces[turn, k, 1])
+                far = jnp.where(indices[s, k] == 0, faces[turn, k, 0], faces[turn, k, 1])
                 far = far.astype(jnp.float32)
                 value = app[s, at, :] - COUPLING * far
                 if turn == 0:
@@ -363,9 +380,15 @@
     return pl.pallas_call(
         functools.partial(kernel, n, coarse_inverse.shape[1] // columns),
         out_shape=jax.ShapeDtypeStruct(field, f32),
-        in_specs=[pl.BlockSpec(memory_space=pl.ANY)] + [vmem] * 6 + [smem] * 3,
+        in_specs=[pl.BlockSpec(memory_space=pltpu.HBM)] * 7 + [smem],
         out_specs=vmem,
         scratch_shapes=[
+            pltpu.VMEM(scaling.shape, f32),
+            pltpu.VMEM((count * points, columns), bf16),
+            pltpu.VMEM(key.shape, jnp.int32),
+            pltpu.VMEM(coarse_inverse.shape, f32),
+            pltpu.VMEM(aero_interp.shape, f32),
+            pltpu.SemaphoreType.DMA((6,)),
             pltpu.VMEM(field, f32),
             pltpu.VMEM((n, SUB_DEV * points, columns), f32),
             pltpu.VMEM(common, f32),
@@ -393,7 +416,7 @@
             pltpu.SemaphoreType.DMA((6,)),
         ],
         compiler_params=pltpu.CompilerParams(
-            collective_id=0, has_side_effects=True, vmem_limit_bytes=44 << 20
+            collective_id=0, has_side_effects=True, vmem_limit_bytes=63 << 20
         ),
     )(
         schur_block,
@@ -403,9 +426,7 @@
         key,
         coarse_inverse,
         aero_interp,
-        partner_slot.T,
-        corner_row,
-        corner_coarse,
+        jnp.concatenate([partner_slot.T, corner_row, corner_coarse], axis=1),
     )
 
 

time: 60.5 us -> 56.7 us (0.937)
  local copies, waits for them, and re-layouts: 8.87 us -> 2.94 us
  other arithmetic: 0.73 us -> 2.1 us
  Pallas kernels: 50.5 us -> 51.4 us
    unnamed x19 -> x1, local copies, waits for them, and re-layouts: 8.76 us -> 2.26 us
    concatenate x0 -> x1, other arithmetic: none -> 1.37 us  [on_device(): jnp.concatenate([partner_slot.T, corner_row, corner_coarse], axis=1)]
    pallas_call x1, Pallas kernels: 50.5 us -> 51.4 us  [on_device(): pl.pallas_call(functools.partial(kernel, n, coarse_inverse.shape[1] // co...]
where the time goes in v4:
time: 56.7 us; the launch traced here: 56.5 us
  Pallas kernels  51.4 us (91%)
  local copies, waits for them, and re-layouts  2.94 us (5%)
  other arithmetic  2.1 us (4%)
    pallas_call x1, Pallas kernels, on_device(): pl.pallas_call(functools.partial(kernel, n, coarse_inverse.shape[1] // co...  51.4 us
    unnamed x1, local copies, waits for them, and re-layouts  2.26 us
    concatenate x1, other arithmetic, on_device(): jnp.concatenate([partner_slot.T, corner_row, corner_coarse], axis=1)  1.37 us

profile of v4, /device:TPU:0, one launch (start us, length us, event | category | flops | bytes accessed | tf_op | source)
XLA Modules:
  0.0 56.5 jit_solution(2331163032268898854)
XLA Ops:
  0.0 0.7 %multiply_bitcast_fusion = s32[64]{0:T(128)S(1)} fusion(s32[64,1]{0,1:T(1,128)} %param.14), kind=kLoop, calls=%fused_computation.2 | loop fusion | flops 64 | bytes 512 | tf_op jit(solution)/shard_map/add | solution.py:373
  0.7 1.4 %pad_add_fusion.indices = s32[2,20]{1,0:T(2,128)} fusion(s32[2,8]{1,0:T(2,128)} %param.18, s32[2,8]{1,0:T(2,128)} %param.17, s32[2,4]{1,0:T(2,128)} %bitcast.5), kind=kLoop, calls=%fused_computation.1 | loop fusion | flops 80 | bytes 320 | tf_op jit(solution)/shard_map/concatenate | solution.py:429
  2.0 0.1 iota_add_fusion
  2.1 0.7 %add.29.key_far = s32[1,256]{1,0:T(1,128)} reshape(s32[64,4]{1,0:T(8,128)S(1)} %iota_add_fusion) | data formatting | bytes 2048 | tf_op jit(solution)/shard_map/add | solution.py:373
  2.8 51.4 %shard_map.100 = f32[2,1024,128]{2,1,0:T(8,128)} custom-call(bf16[2,512,1024]{2,1,0:T(8,128)(2,1)} %schur.1, f32[2,1024]{1,0:T(2,128)} %scaling_far.1, f32[2,1024,128]{2,1,0:T(8,128)} %gravity_far.1, bf16[256,128]{1,0:T(8,128)(2,1)} %bitcast.4, s32[1,256]{1,0:T(1,128)} %add.29.key_far, f32[8,128]{1,0:T(8,128)} %inverse_far.1, f32[4,1024]{1,0:T(4,128)} %interp_far.1, ...), custom_call_target="tpu_custom_call" | custom-call | tf_op jit(solution)/shard_map/pallas_call | solution.py:380
  54.2 2.3 %copy.12 = f32[2,1024,128]{2,1,0:T(8,128)} copy(f32[2,1024,128]{2,1,0:T(8,128)} %shard_map.100) | data formatting | bytes 2097152
